TPU v7x, 128 devices: a whole 4x4x4 slice. The times are simulated.
128 devices in a mesh: gx: 4 (over y), gy: 4 (over x), zt: 8 (over z, core).
Axes of the slice: x: 4, y: 4, z: 4, core: 2. Of those that a mesh axis runs over, the one named last changes fastest.
Arguments:
- gauge_links: float32 [4, 3, 3, 2, 2, 32, 64, 512], P(None, None, None, None, None, 'zt', 'gy', 'gx'), may hold values from -2 to 2, as said below
- slab_bounds: int32 [2, 9], replicated, may hold values from 0 to 32, as said below
Outputs:
- file_links: float32 [4, 3, 3, 2, 2, 48, 4, 4, 4, 4, 128], P(None, None, None, None, None, 'zt', None, 'gx', None, 'gy')
- plaquette: float32 [2, 32, 64, 512], P(None, 'zt', 'gy', 'gx')
- plaquette_mean: float32 [], replicated
Inputs may be any that keep to these rules, and one draw needn't show every extreme that they name: `gauge_links`: every link matrix is strictly diagonally dominant by rows. Each row slab_bounds[t] rises, starts at 0 and ends at 32; each interior slab_bounds[t, w] lies exactly 1 plane from w * 4, on one side in even timeslices and on the other in odd ones; some writer's slab holds 6 z planes.
All inputs are finite; a program needn't handle non-finite values.
Results may differ from a plain program's by a relative error of at most 0.0003.
Values sent between devices are 32-bit elements; how exact they have to be, the bound alone decides.
No kernel may reach another device: no remote copies, remote signals or barrier semaphores. Data moves between devices by JAX's collectives and lax.ppermute only.
A program may use at most 128 MiB of HBM per device.

v0:
```python
import jax
import jax.numpy as jnp
from jax import lax
from jax.experimental import pallas as pl
from jax.experimental.pallas import tpu as pltpu
from jax.sharding import PartitionSpec as P

VMEM_LIMIT = 24 * 1024 * 1024
CROSS = ((1, 2), (2, 0), (0, 1))


def passed_along(value, axis, by):
    count = lax.axis_size(axis)
    return lax.ppermute(value, axis, [(i, (i + by) % count) for i in range(count)])


def times(a, b):
    return (a[0] * b[0] - a[1] * b[1], a[0] * b[1] + a[1] * b[0])


def times_conj(a, b):
    return (a[0] * b[0] + a[1] * b[1], a[1] * b[0] - a[0] * b[1])


def minus(a, b):
    return (a[0] - b[0], a[1] - b[1])


def scaled(a, s):
    return (a[0] * s, a[1] * s)


def square(a):
    return a[0] * a[0] + a[1] * a[1]


def last_row(u, v):
    rows = []
    for b, c in CROSS:
        x = minus(times(u[b], v[c]), times(u[c], v[b]))
        rows.append((x[0], -x[1]))
    return rows


def unit_rows(r1, r2):
    n = lax.rsqrt(square(r1[0]) + square(r1[1]) + square(r1[2]))
    u = [scaled(x, n) for x in r1]
    terms = [times_conj(y, x) for x, y in zip(u, r2)]
    c = (terms[0][0] + terms[1][0] + terms[2][0], terms[0][1] + terms[1][1] + terms[2][1])
    v = [minus(y, times(c, x)) for x, y in zip(u, r2)]
    n = lax.rsqrt(square(v[0]) + square(v[1]) + square(v[2]))
    v = [scaled(x, n) for x in v]
    return [u, v, last_row(u, v)]


def angle_value(a):
    t = a[1] / (jnp.abs(a[0]) + jnp.abs(a[1]))
    return jnp.where(a[0] < 0.0, 2.0 - t, t)


def angle_point(t):
    back = t > 1.0
    y = jnp.where(back, 2.0 - t, t)
    x = 1.0 - jnp.abs(y)
    x = jnp.where(back, -x, x)
    return (x, y), x * x + y * y


def to_parameters(r1, r2):
    inverse = 1.0 / square(r1[0])
    p1 = scaled(times_conj(r1[1], r1[0]), inverse)
    p2 = scaled(times_conj(r1[2], r1[0]), inverse)
    s1 = minus(r2[1], times(r2[0], p1))
    s2 = minus(r2[2], times(r2[0], p2))
    q = scaled(times_conj(s2, s1), 1.0 / square(s1))
    return [p1[0], p1[1], p2[0], p2[1], q[0], q[1], angle_value(r1[0]), angle_value(s1)]


def from_parameters(values):
    p1 = (values[0], values[1])
    p2 = (values[2], values[3])
    q = (values[4], values[5])
    size = 1.0 + square(p1) + square(p2)
    g = times_conj(q, p2)
    g = (g[0] + p1[0], g[1] - p1[1])
    gp1 = times(g, p1)
    gp2 = times(g, p2)
    v = [(-g[0], -g[1]), (size - gp1[0], -gp1[1]), (size * q[0] - gp2[0], size * q[1] - gp2[1])]
    a, a2 = angle_point(values[6])
    a = scaled(a, lax.rsqrt(a2 * size))
    b, b2 = angle_point(values[7])
    b = scaled(b, lax.rsqrt(b2 * (square(v[0]) + square(v[1]) + square(v[2]))))
    u = [a, times(a, p1), times(a, p2)]
    v = [times(b, x) for x in v]
    k = scaled(times(a, b), size)
    first = times(k, minus(times(p1, q), p2))
    second = times(k, q)
    return [u, v, [(first[0], -first[1]), (-second[0], second[1]), (k[0], -k[1])]]


ENTRIES = [(r, c, i) for r in range(2) for c in range(3) for i in range(2)]


def pairs(parts):
    return [(parts[2 * i], parts[2 * i + 1]) for i in range(len(parts) // 2)]


def moving_times(bounds_ref, w):
    top = jnp.where(bounds_ref[0, w + 1] < 4 * w + 4, 0, 1)
    bottom = jnp.where(bounds_ref[0, w] > 4 * w, 0, 1)
    return top, bottom


def turned(x, lane):
    odd = (lane & 32) != 0
    far = (lane & 64) != 0
    x = [jnp.where(odd, x[(d + 1) % 4], x[d]) for d in range(4)]
    x = [jnp.where(far, x[(d + 2) % 4], x[d]) for d in range(4)]
    x = [pltpu.roll(x[d], 32 * d, 1) if d else x[d] for d in range(4)]
    x = [jnp.where(odd, x[(1 - g) % 4], x[-g % 4]) for g in range(4)]
    return [jnp.where(far, x[(g + 2) % 4], x[g]) for g in range(4)]


def encode_planes(rows, out, stride):
    lane = lax.broadcasted_iota(jnp.int32, (8, 128), 1)
    low = lax.broadcasted_iota(jnp.int32, (8, 128), 0) < 4
    by_row = []
    for r in range(4):
        parts = pairs([rows[pl.ds(c * 32 + r, 8, stride=4), :] for c in range(12)])
        by_row.append(to_parameters(parts[:3], parts[3:]))
    for p in range(8):
        z = turned([by_row[r][p] for r in range(4)], lane)
        for h in (0, 1):
            first = jnp.where(low, z[2 * h], pltpu.roll(z[2 * h + 1], 4, 0))
            second = jnp.where(low, pltpu.roll(z[2 * h], 4, 0), z[2 * h + 1])
            out[pl.ds(h * 8 * stride + p, 8, stride=stride), :] = first
            out[pl.ds(h * 8 * stride + 8 + p, 8, stride=stride), :] = second


def block_half(h):
    return pl.multiple_of(8 * (h ^ (lax.axis_index("zt") % 2)), 8)


def encode_kernel(taken, out_ref, given, out_sem):
    def copy_out(step, h):
        at = pl.ds(pl.multiple_of((step % 3) * 16, 16), 16)
        return pltpu.make_async_copy(
            given.at[step, pl.ds(8 * h, 8)], out_ref.at[pl.ds(block_half(h), 8), step // 3, at], out_sem.at[h, step]
        )

    def one(step, carry):
        encode_planes(taken.at[step].reshape(12 * 32, 128), given.at[step].reshape(16 * 16, 128), 16)
        copy_out(step, 0).start()
        copy_out(step, 1).start()
        return carry

    lax.fori_loop(0, 12, one, 0)
    for step in range(12):
        copy_out(step, 0).wait()
        copy_out(step, 1).wait()


def encoded(taken):
    return pl.pallas_call(
        encode_kernel,
        in_specs=[pl.BlockSpec(memory_space=pltpu.VMEM)],
        out_specs=pl.BlockSpec(memory_space=pltpu.HBM),
        out_shape=pltpu.HBM((16, 4, 48, 128), jnp.float32),
        scratch_shapes=[pltpu.VMEM((12, 16, 16, 128), jnp.float32), pltpu.SemaphoreType.DMA((2, 12))],
        compiler_params=pltpu.CompilerParams(vmem_limit_bytes=VMEM_LIMIT),
    )(taken)


class ShiftedRows:
    def __init__(self, ref, by):
        self.ref = ref
        self.by = by

    def __setitem__(self, at, value):
        self.ref[pl.ds(self.by + at[0].start, at[0].size, stride=at[0].stride), :] = value


def encode_rest_kernel(rest, total_ref, out_ref, given, out_sem):
    out = given.reshape(16 * 72, 128)
    for n in range(16):
        given[n, pl.ds(64, 8), :] = total_ref[...]

    def copy_out(m, size, h):
        at = pl.ds(pl.multiple_of(m * 16, 8), size)
        return pltpu.make_async_copy(
            given.at[pl.ds(8 * h, 8), at], out_ref.at[pl.ds(block_half(h), 8), at], out_sem.at[h, m]
        )

    copy_out(4, 8, 0).start()
    copy_out(4, 8, 1).start()

    def one(m, carry):
        encode_planes(rest.at[m].reshape(12 * 32, 128), ShiftedRows(out, m * 16), 72)
        copy_out(m, 16, 0).start()
        copy_out(m, 16, 1).start()
        return carry

    lax.fori_loop(0, 4, one, 0)
    for h in range(2):
        for m in range(4):
            copy_out(m, 16, h).wait()
        copy_out(4, 8, h).wait()


def encoded_rest(rest, total):
    return pl.pallas_call(
        encode_rest_kernel,
        in_specs=[pl.BlockSpec(memory_space=pltpu.VMEM)] * 2,
        out_specs=pl.BlockSpec(memory_space=pltpu.HBM),
        out_shape=pltpu.HBM((16, 72, 128), jnp.float32),
        scratch_shapes=[pltpu.VMEM((16, 72, 128), jnp.float32), pltpu.SemaphoreType.DMA((2, 5))],
        compiler_params=pltpu.CompilerParams(vmem_limit_bytes=VMEM_LIMIT),
    )(rest, total)


def take_kernel(links_ref, x_ref, y_ref, z_ref, taken, rest, in_sem, rest_sem, z_sem):
    def copy_in(m, pair):
        if pair == 2:
            source = links_ref.at[m, pl.ds(0, 2), :, :, :, 3]
        else:
            source = links_ref.at[m, pl.ds(0, 2), :, :, pair, pl.ds(0, 2)]
        return pltpu.make_async_copy(source, taken.at[3 * m + pair], in_sem.at[3 * m + pair])

    def copy_rest(m):
        return pltpu.make_async_copy(links_ref.at[m, pl.ds(0, 2), :, :, :, 2], rest.at[m], rest_sem.at[m])

    def copies(m):
        return [copy_in(m, pair) for pair in range(3)] + [copy_rest(m)]

    copy_z = pltpu.make_async_copy(links_ref.at[pl.ds(0, 2), pl.ds(0, 2), :, :, :, 0], z_ref, z_sem)
    order = (2, 1, 0, 3)
    for m in order:
        for copy in copies(m):
            copy.start()
    copy_z.start()

    def rows(m, r, c, i, k, start, size):
        t, z = k // 4, k % 4
        at = pl.ds(start, size)
        if z == 2:
            return rest[m, r, c, i, t, at, :]
        if z == 3:
            return taken[3 * m + 2, r, c, i, t, at, :]
        return taken[3 * m + t, r, c, i, z, at, :]

    def row_face(m):
        parts = pairs([jnp.concatenate([rows(m, *e, k, 0, 1) for k in range(8)], axis=0) for e in ENTRIES])
        for p, value in enumerate(to_parameters(parts[:3], parts[3:])):
            y_ref[m // 2, p] = value

    lane = lax.broadcasted_iota(jnp.int32, (8, 128), 1)
    got = [None] * 3

    def column_face(m):
        for e, entry in enumerate(ENTRIES):
            n = 12 * (m - 1) + e
            for k in range(8):
                for h in range(2):
                    at = 16 * (n % 8) + 2 * k + h
                    value = rows(m, *entry, k, 8 * h, 8)
                    value = pltpu.roll(value, at, 1) if at else value
                    got[n // 8] = value if got[n // 8] is None else jnp.where(lane == at, value, got[n // 8])

    for m in order:
        for copy in copies(m):
            copy.wait()
        if m in (1, 2):
            column_face(m)
        if m in (0, 2):
            row_face(m)
    for n in range(3):
        x_ref[n] = got[n]
    copy_z.wait()


def taken_links(links):
    kept = pl.BlockSpec(memory_space=pltpu.VMEM)
    return pl.pallas_call(
        take_kernel,
        in_specs=[pl.BlockSpec(memory_space=pltpu.HBM)],
        out_specs=[kept] * 5,
        out_shape=[
            pltpu.VMEM((3, 8, 128), jnp.float32),
            pltpu.VMEM((2, 8, 8, 128), jnp.float32),
            pltpu.VMEM((2, 2, 3, 2, 2, 16, 128), jnp.float32),
            pltpu.VMEM((12, 2, 3, 2, 2, 16, 128), jnp.float32),
            pltpu.VMEM((4, 2, 3, 2, 2, 16, 128), jnp.float32),
        ],
        scratch_shapes=[
            pltpu.SemaphoreType.DMA((12,)),
            pltpu.SemaphoreType.DMA((4,)),
            pltpu.SemaphoreType.DMA,
        ],
        compiler_params=pltpu.CompilerParams(vmem_limit_bytes=VMEM_LIMIT),
    )(links)


def flat_rows(matrix):
    return [part for row in matrix for entry in row for part in entry]


def product_trace(a, b, c, d):
    total = None
    for i in range(3):
        for j in range(3):
            one = two = None
            for k in range(3):
                x = times(a[i][k], b[k][j])
                y = times(c[i][k], d[k][j])
                one = x if one is None else (one[0] + x[0], one[1] + x[1])
                two = y if two is None else (two[0] + y[0], two[1] + y[1])
            term = one[0] * two[0] + one[1] * two[1]
            total = term if total is None else total + term
    return total


class Sites:
    def __init__(self, unit, x_edge, y_edge, z_edge, out_ref):
        self.unit, self.x_edge, self.y_edge, self.z_edge = unit, x_edge, y_edge, z_edge
        self.out_ref = out_ref
        self.last_lane = lax.broadcasted_iota(jnp.int32, (8, 128), 1) == 127
        self.first_row = lax.broadcasted_iota(jnp.int32, (8, 128), 0) == 0

    def matrix(self, parts):
        parts = pairs(parts)
        return [parts[3 * i : 3 * i + 3] for i in range(3)]

    def here(self, m, t, z, h):
        return self.matrix([self.unit[m, c, t, z, pl.ds(8 * h, 8), :] for c in range(18)])

    def next_x(self, m, t, z, h):
        got = []
        for c in range(18):
            value = pltpu.roll(self.unit[m, c, t, z, pl.ds(8 * h, 8), :], 127, 1)
            beyond = pltpu.roll(self.x_edge[m - 1, c], 127 - 2 * (4 * t + z) - h, 1)
            got.append(jnp.where(self.last_lane, beyond, value))
        return self.matrix(got)

    def next_y(self, m, t, z, h):
        if h == 0:
            return self.matrix([self.unit[m, c, t, z, pl.ds(1, 8), :] for c in range(18)])
        got = []
        for c in range(18):
            value = self.unit[m, c, t, z, pl.ds(8, 8), :]
            beyond = self.y_edge[m // 2, c, pl.ds(4 * t + z, 1), :]
            value = jnp.where(self.first_row, beyond, value)
            got.append(pltpu.roll(value, 7, 0))
        return self.matrix(got)

    def next_z(self, m, t, z, h):
        if self.z_edge is None:
            return self.here(m, t, z + 1, h)
        return self.matrix([self.z_edge[m, c, t, pl.ds(8 * h, 8), :] for c in range(18)])

    def plane(self, t, z):
        total = None
        for h in range(2):
            at = (t, z, h)
            value = product_trace(self.here(0, *at), self.next_x(1, *at), self.here(1, *at), self.next_y(0, *at))
            value = value + product_trace(
                self.here(0, *at), self.next_x(2, *at), self.here(2, *at), self.next_z(0, *at)
            )
            value = value + product_trace(
                self.here(1, *at), self.next_y(2, *at), self.here(2, *at), self.next_z(1, *at)
            )
            value = value * (1.0 / 9.0)
            self.out_ref[t, z, pl.ds(8 * h, 8), :] = value
            total = value if total is None else total + value
        return total


def inner_kernel(links_ref, x_ref, y_ref, out_ref, sum_ref, unit, x_edge, y_edge, taken, sem):
    def copy_in(step):
        return pltpu.make_async_copy(
            links_ref.at[step // 2, pl.ds(0, 2), :, :, step % 2], taken.at[step], sem.at[step]
        )

    for step in range(6):
        copy_in(step).start()
    for m in range(2):
        for c, value in enumerate(flat_rows(from_parameters([y_ref[m, p] for p in range(8)]))):
            y_edge[m, c] = value
        parts = []
        for e in range(12):
            n = 12 * m + e
            value = x_ref[n // 8]
            parts.append(pltpu.roll(value, 128 - 16 * (n % 8), 1) if n % 8 else value)
        parts = pairs(parts)
        for c, value in enumerate(flat_rows(unit_rows(parts[:3], parts[3:]))):
            x_edge[m, c] = value

    def own(step, carry):
        part = step // 4
        z = step % 4

        @pl.when(z == 0)
        def _():
            copy_in(part).wait()

        for h in range(2):
            at = pl.ds(8 * h, 8)
            parts = pairs([taken[part, r, c, i, z, at, :] for r, c, i in ENTRIES])
            for c, value in enumerate(flat_rows(unit_rows(parts[:3], parts[3:]))):
                unit[part // 2, c, part % 2, z, at, :] = value
        return carry

    lax.fori_loop(0, 24, own, 0)
    sites = Sites(unit, x_edge, y_edge, None, out_ref)
    zero = jnp.zeros((8, 128), jnp.float32)
    sum_ref[...] = lax.fori_loop(0, 6, lambda step, total: total + sites.plane(step // 3, step % 3), zero)


def inner_plaquettes(links, x_face, y_face):
    kept = pl.BlockSpec(memory_space=pltpu.VMEM)
    return pl.pallas_call(
        inner_kernel,
        in_specs=[pl.BlockSpec(memory_space=pltpu.HBM)] + [kept] * 2,
        out_specs=[kept] * 5,
        out_shape=[
            pltpu.VMEM((2, 4, 16, 128), jnp.float32),
            pltpu.VMEM((8, 128), jnp.float32),
            pltpu.VMEM((3, 18, 2, 4, 16, 128), jnp.float32),
            pltpu.VMEM((2, 18, 8, 128), jnp.float32),
            pltpu.VMEM((2, 18, 8, 128), jnp.float32),
        ],
        scratch_shapes=[
            pltpu.VMEM((6, 2, 3, 2, 4, 16, 128), jnp.float32),
            pltpu.SemaphoreType.DMA((6,)),
        ],
        compiler_params=pltpu.CompilerParams(vmem_limit_bytes=VMEM_LIMIT),
    )(links, x_face, y_face)


def outer_kernel(inner_ref, part_ref, unit, x_edge, y_edge, z_ref, out_ref, sum_ref, z_edge):
    for t in range(2):
        for z in range(3):
            out_ref[t, z] = inner_ref[t, z]

    def above(step, carry):
        m = step // 2
        t = step % 2
        for h in range(2):
            at = pl.ds(8 * h, 8)
            parts = pairs([z_ref[m, r, c, i, t, at, :] for r, c, i in ENTRIES])
            for c, value in enumerate(flat_rows(unit_rows(parts[:3], parts[3:]))):
                z_edge[m, c, t, at, :] = value
        return carry

    lax.fori_loop(0, 4, above, 0)
    sites = Sites(unit, x_edge, y_edge, z_edge, out_ref)
    total = lax.fori_loop(0, 2, lambda t, total: total + sites.plane(t, 3), part_ref[...])
    sum_ref[...] = jnp.broadcast_to(jnp.sum(total, keepdims=True), (8, 128))


def outer_plaquettes(inner, part, unit, x_edge, y_edge, z_face):
    kept = pl.BlockSpec(memory_space=pltpu.VMEM)
    return pl.pallas_call(
        outer_kernel,
        in_specs=[kept] * 6,
        out_shape=[
            jax.ShapeDtypeStruct((2, 4, 16, 128), jnp.float32),
            jax.ShapeDtypeStruct((8, 128), jnp.float32),
        ],
        scratch_shapes=[pltpu.VMEM((2, 18, 2, 16, 128), jnp.float32)],
        compiler_params=pltpu.CompilerParams(vmem_limit_bytes=VMEM_LIMIT),
    )(inner, part, unit, x_edge, y_edge, z_face)


def put_planes(sources, bounds, placed, out_ref, planes, sem):
    def copy_out(places, part, m):
        t, j = places[part]
        return pltpu.make_async_copy(planes.at[part, m], out_ref.at[pl.ds(18 * m, 18), t, j], sem.at[part, m])

    def decode(part, m):
        rows, stride, start, step, half = sources[part]
        for h in range(2):
            at = half(h) * stride + start + m * step
            values = [rows[pl.ds(at + p, 8, stride=stride), :] for p in range(8)]
            for c, value in enumerate(flat_rows(from_parameters(values))):
                planes[part, m, c, pl.ds(8 * h, 8), :] = value

    parts = range(len(sources))
    for part in parts:
        decode(part, 0)
    if bounds is not None:
        bounds.wait()
    places = placed()
    for part in parts:
        copy_out(places, part, 0).start()

    def one(m, carry):
        for part in parts:
            decode(part, m)
            copy_out(places, part, m).start()
        return carry

    lax.fori_loop(1, 4, one, 0)
    for m in range(4):
        for part in parts:
            copy_out(places, part, m).wait()


PLANE_SCRATCH = [
    pltpu.VMEM((4, 4, 18, 16, 128), jnp.float32),
    pltpu.SemaphoreType.DMA((4, 4)),
    pltpu.SMEM((2, 9), jnp.int32),
    pltpu.SemaphoreType.DMA,
]


def decode_kernel(bounds_in, own_ref, out_ref, planes, sem, bounds_ref, bounds_sem, zeros, zero_sem):
    bounds = pltpu.make_async_copy(bounds_in, bounds_ref, bounds_sem)
    bounds.start()
    w = lax.axis_index("zt")
    zeros[...] = jnp.zeros((18, 16, 128), jnp.float32)

    def fill(t, j, m):
        return pltpu.make_async_copy(zeros, out_ref.at[pl.ds(18 * m, 18), t, j], zero_sem.at[t, j - 2])

    def every_empty(act):
        for t in range(2):
            depth = bounds_ref[t, w + 1] - bounds_ref[t, w]
            for j in range(2, 6):

                @pl.when(j >= depth)
                def _(t=t, j=j):
                    for m in range(4):
                        act(fill(t, j, m))

    bounds.wait()
    every_empty(lambda copy: copy.start())
    top, bottom = moving_times(bounds_ref, w)
    rows = own_ref.reshape(16 * 192, 128)
    planes_in = ((1 - top, 3, 5 - top), (1 - bottom, 0, 2 - 2 * bottom), (0, 1, 1), (1, 1, 3))
    sources = [(rows, 192, 8 * slot, 48, block_half) for t, z, slot in planes_in]
    places = [(t, z + 4 * w - bounds_ref[t, w]) for t, z, slot in planes_in]
    put_planes(sources, None, lambda: places, out_ref, planes, sem)
    every_empty(lambda copy: copy.wait())


def decoded(bounds, own):
    return pl.pallas_call(
        decode_kernel,
        in_specs=[pl.BlockSpec(memory_space=pl.ANY), pl.BlockSpec(memory_space=pltpu.VMEM)],
        out_specs=pl.BlockSpec(memory_space=pltpu.HBM),
        out_shape=jax.ShapeDtypeStruct((72, 2, 6, 16, 128), jnp.float32),
        scratch_shapes=PLANE_SCRATCH
        + [pltpu.VMEM((18, 16, 128), jnp.float32), pltpu.SemaphoreType.DMA((2, 4))],
        compiler_params=pltpu.CompilerParams(vmem_limit_bytes=VMEM_LIMIT),
    )(bounds, own)


def cut_kernel(bounds_ref, own_ref, first_ref, second_ref):
    w = lax.axis_index("zt")
    top, bottom = moving_times(bounds_ref, w)
    even = w % 2 == 0
    top = 32 + 8 * top
    bottom = 16 * bottom
    first = pl.multiple_of(jnp.where(even, top, bottom), 8)
    second = pl.multiple_of(jnp.where(even, bottom, top), 8)
    for h in range(2):
        here = pl.ds(8 * h, 8)
        there = pl.ds(block_half(h), 8)
        for m in range(4):
            first_ref[here, m] = own_ref[there, m, pl.ds(first, 8), :]
            second_ref[here, m] = own_ref[there, m, pl.ds(second, 8), :]


def cut_planes(bounds, own):
    return pl.pallas_call(
        cut_kernel,
        in_specs=[pl.BlockSpec(memory_space=pltpu.SMEM), pl.BlockSpec(memory_space=pltpu.VMEM)],
        out_shape=[jax.ShapeDtypeStruct((16, 4, 8, 128), jnp.float32)] * 2,
        compiler_params=pltpu.CompilerParams(vmem_limit_bytes=VMEM_LIMIT),
    )(bounds, own)


def rest_kernel(
    count,
    bounds_in,
    first_ref,
    second_ref,
    rest_ref,
    whole_ref,
    out_ref,
    mean_ref,
    planes,
    sem,
    bounds_ref,
    bounds_sem,
    mean,
    mean_sem,
):
    bounds = pltpu.make_async_copy(bounds_in, bounds_ref, bounds_sem)
    bounds.start()
    w = lax.axis_index("zt")
    totals = []
    for h in range(2):
        part = rest_ref[block_half(h), pl.ds(64, 8), :]
        for n in range(1, 8):
            part = part + rest_ref[block_half(h) + n, pl.ds(64, 8), :]
        totals.append(part)
    mean[0, 0] = jnp.max(totals[0] + totals[1]) * (1.0 / count)
    mean_out = pltpu.make_async_copy(mean, mean_ref, mean_sem)
    mean_out.start()
    rows = rest_ref.reshape(16 * 72, 128)
    sources = [(ref.reshape(16 * 32, 128), 32, 0, 8, lambda h: 8 * h) for ref in (first_ref, second_ref)]
    sources += [(rows, 72, 8 * t, 16, block_half) for t in range(2)]

    def placed():
        top, bottom = moving_times(bounds_ref, w)
        even = w % 2 == 0
        low_time = jnp.where(w == 0, bottom, 1 - bottom)
        high_time = jnp.where(w == 7, top, 1 - top)
        high_at = jnp.where(w == 7, 3, 4) + 4 * w - bounds_ref[high_time, w]
        low_at = jnp.int32(0)
        places = [
            (jnp.where(even, high_time, low_time), jnp.where(even, high_at, low_at)),
            (jnp.where(even, low_time, high_time), jnp.where(even, low_at, high_at)),
        ]
        return places + [(t, 2 + 4 * w - bounds_ref[t, w]) for t in range(2)]

    put_planes(sources, bounds, placed, out_ref, planes, sem)
    mean_out.wait()


def with_rest(bounds, first, second, rest, whole, count):
    kept = pl.BlockSpec(memory_space=pltpu.VMEM)
    there = pl.BlockSpec(memory_space=pltpu.HBM)
    return pl.pallas_call(
        lambda *refs: rest_kernel(count, *refs),
        in_specs=[pl.BlockSpec(memory_space=pl.ANY)] + [kept] * 3 + [there],
        out_specs=[there, there],
        out_shape=[
            jax.ShapeDtypeStruct((72, 2, 6, 16, 128), jnp.float32),
            jax.ShapeDtypeStruct((1, 1), jnp.float32),
        ],
        input_output_aliases={4: 0},
        scratch_shapes=PLANE_SCRATCH + [pltpu.SMEM((1, 1), jnp.float32), pltpu.SemaphoreType.DMA],
        compiler_params=pltpu.CompilerParams(vmem_limit_bytes=VMEM_LIMIT),
    )(bounds, first, second, rest, whole)


def summed(value, steps):
    for axis, by in steps:
        count = lax.axis_size(axis)
        value = value + lax.ppermute(value, axis, [(i, i ^ by) for i in range(count)])
    return value


def spread(payload):
    places = [(gx, gy) for gy in range(4) for gx in range(4)]
    groups = [[(gx * 4 + gy) * 8 + w for gx, gy in places[8 * (w % 2) :] + places[: 8 * (w % 2)]] for w in range(8)]
    return lax.all_to_all(
        payload, ("gx", "gy", "zt"), split_axis=0, concat_axis=0, axis_index_groups=groups, tiled=True
    )


def local(links, bounds):
    held = pltpu.with_memory_space_constraint(links, pltpu.HBM)
    x_face, y_face, z_face, taken, rest = taken_links(held)
    y_face = passed_along(y_face, "gy", -1)
    x_face = passed_along(x_face, "gx", -1)
    payload = encoded(taken)
    payload, links, x_face, y_face, z_face = lax.optimization_barrier((payload, links, x_face, y_face, z_face))
    held = pltpu.with_memory_space_constraint(links, pltpu.HBM)
    moved = spread(payload)
    z_face = passed_along(z_face, "zt", -1)
    plaquette, total = outer_plaquettes(*inner_plaquettes(held, x_face, y_face), z_face)
    total = summed(total, (("zt", 1), ("zt", 2), ("zt", 6)))
    rest = encoded_rest(rest, total)
    moved, rest = lax.optimization_barrier((moved, rest))
    moved_rest = spread(rest)
    first, second = cut_planes(bounds, moved)
    first = lax.ppermute(first, "zt", [(i, i ^ 1) for i in range(8)])
    second = lax.ppermute(second, "zt", [(0, 0), (7, 7)] + [(i, (i + 1 ^ 1) - 1) for i in range(1, 7)])
    file_links = decoded(bounds, moved)
    file_links, mean = with_rest(bounds, first, second, moved_rest, file_links, plaquette.size * 128)
    return file_links.reshape(4, 3, 3, 2, 2, 6, 4, 1, 4, 1, 128), plaquette, mean[0, 0]


def solution(mesh):
    in_specs = (P(None, None, None, None, None, "zt", "gy", "gx"), P())
    out_specs = (
        P(None, None, None, None, None, "zt", None, "gx", None, "gy", None),
        P(None, "zt", "gy", "gx"),
        P(),
    )
    return jax.shard_map(local, mesh=mesh, in_specs=in_specs, out_specs=out_specs, check_vma=False)
```

profile of v0, /device:TPU:0, one launch (start us, length us, event | category | flops | bytes accessed | tf_op | source)
XLA Modules:
  0.0 55.8 jit_solution(8723176042506129708)
XLA Ops:
  0.6 2.3 %shard_map.49 = (f32[3,8,128]{2,1,0:T(8,128)S(1)}, f32[2,8,8,128]{3,2,1,0:T(8,128)S(1)}, f32[2,2,3,2,2,16,128]{6,5,4,3,2,1,0:T(8,128)S(1)}, f32[12,2,3,2,2,16,12...) custom-call(f32[4,3,3,2,2,4,16,128]{7,6,5,4,3,2,1,0:T(8,128)} %links_ref.2), custom_call_target="tpu_custom_call" | custom-call | tf_op jit(solution)/shard_map/pallas_call | solution.py:283
  2.9 2.9 %collective-permute-start.1 = (f32[2,8,8,128]{3,2,1,0:T(8,128)S(1)}, f32[2,8,8,128]{3,2,1,0:T(8,128)S(1)}, u32[]{:S(2)}, u32[]{:S(2)}) collective-permute-start(f32[2,8,8,128]{3,2,1,0:T(8,128)S(1)} %get-tuple-element.28), channel_id=1, source_target_pairs={{0,24},{8,0},{16,8},{24,16},{1,25},{9,1},{17,9},{25,17},{2,26},{10... | collective-permute-start | bytes 196616 | tf_op jit(solution)/shard_map/ppermute | solution.py:14
  5.9 3.0 %collective-permute-start = (f32[3,8,128]{2,1,0:T(8,128)S(1)}, f32[3,8,128]{2,1,0:T(8,128)S(1)}, u32[]{:S(2)}, u32[]{:S(2)}) collective-permute-start(f32[3,8,128]{2,1,0:T(8,128)S(1)} %get-tuple-element.27), channel_id=1, source_target_pairs={{0,96},{32,0},{64,32},{96,64},{1,97},{33,1},{65,33},{97,65},{2,98}... | collective-permute-start | bytes 36872 | tf_op jit(solution)/shard_map/ppermute | solution.py:14
  8.9 2.4 %shard_map.50 = f32[16,4,48,128]{3,2,1,0:T(8,128)} custom-call(f32[12,2,3,2,2,16,128]{6,5,4,3,2,1,0:T(8,128)S(1)} %get-tuple-element.26.taken), custom_call_target="tpu_custom_call" | custom-call | tf_op jit(solution)/shard_map/pallas_call | solution.py:164
  11.3 0.0 collective-permute-done.x_ref
  11.3 0.0 collective-permute-done.1.y_ref
  11.3 4.1 %all-to-all-start = ((f32[16,4,48,128]{3,2,1,0:T(8,128)}), f32[16,4,48,128]{3,2,1,0:T(8,128)S(1)}, u32[]{:S(2)}, u32[]{:S(2)}) async-start(f32[16,4,48,128]{3,2,1,0:T(8,128)} %shard_map.50), calls=%async_computation | async-start | bytes 3145728 | tf_op jit(solution)/shard_map/all_to_all | solution.py:659
  15.4 4.1 %collective-permute-start.2 = (f32[2,2,3,2,2,16,128]{6,5,4,3,2,1,0:T(8,128)S(1)}, f32[2,2,3,2,2,16,128]{6,5,4,3,2,1,0:T(8,128)S(1)}, u32[]{:S(2)}, u32[]{:S(2)}) collective-permute-start(f32[2,2,3,2,2,16,128]{6,5,4,3,2,1,0:T(8,128)S(1)} %get-tuple-element.40), channel_id=1, source_target_pairs={{0,7},{1,0},{2,1},{3,2},{4,3},{5,4},{6,5},{7,6},{8,15},{9,8},{10,9... | collective-permute-start | bytes 1179656 | tf_op jit(solution)/shard_map/ppermute | solution.py:14
  19.5 5.2 %shard_map.51 = (f32[2,4,16,128]{3,2,1,0:T(8,128)S(1)}, f32[8,128]{1,0:T(8,128)S(1)}, f32[3,18,2,4,16,128]{5,4,3,2,1,0:T(8,128)S(1)}, f32[2,18,8,128]{3,2,1,0:T(8,128)S(1)}, f32[2,18,8,128]{3,2,1,0:T(8,128)S(1)}) custom-call(f32[4,3,3,2,2,4,16,128]{7,6,5,4,3,2,1,0:T(8,128)} %links_ref.2, f32[3,8,128]{2,1,0:T(8,128)S(1)} %collective-permute-done.x_ref, ...), custom_call_target="tpu_custom_call" | custom-call | tf_op jit(solution)/shard_map/pallas_call | solution.py:420
  24.7 0.0 copy-start
  24.7 0.1 collective-permute-done.2.z_ref
  24.8 1.8 %shard_map.52 = (f32[2,4,16,128]{3,2,1,0:T(8,128)}, f32[8,128]{1,0:T(8,128)S(1)}) custom-call(f32[2,4,16,128]{3,2,1,0:T(8,128)S(1)} %get-tuple-element.35.inner_ref, f32[8,128]{1,0:T(8,128)S(1)} %get-tuple-element.36.part_ref, f32[3,18,2,4,16,128]{5,4,3,2,1,0:T(8,128)S(1)} %get-tuple-element.37.unit, f32[2,18,8,128]{3,2,1,0:T(8,128)S(1)} %get-tuple-element.38.x_edge, ...), custom_call_target="tpu_custom_call" | custom-call | tf_op jit(solution)/shard_map/pallas_call | solution.py:462
  26.6 0.0 collective-permute-start.3
  26.6 1.2 %collective-permute-done.3 = f32[8,128]{1,0:T(8,128)S(1)} collective-permute-done((f32[8,128]{1,0:T(8,128)S(1)}, f32[8,128]{1,0:T(8,128)S(1)}, u32[]{:S(2)}, u32[]{:S(2)}) %collective-permute-start.3) | collective-permute-done | bytes 4128 | tf_op jit(solution)/shard_map/ppermute | solution.py:652
  27.8 0.1 collective-permute-start.4
  27.9 3.5 %collective-permute-done.4 = f32[8,128]{1,0:T(8,128)S(1)} collective-permute-done((f32[8,128]{1,0:T(8,128)S(1)}, f32[8,128]{1,0:T(8,128)S(1)}, u32[]{:S(2)}, u32[]{:S(2)}) %collective-permute-start.4) | collective-permute-done | bytes 4128 | tf_op jit(solution)/shard_map/ppermute | solution.py:652
  31.4 3.5 %collective-permute-start.5 = (f32[8,128]{1,0:T(8,128)S(1)}, f32[8,128]{1,0:T(8,128)S(1)}, u32[]{:S(2)}, u32[]{:S(2)}) collective-permute-start(f32[8,128]{1,0:T(8,128)S(1)} %add.10), channel_id=1, source_target_pairs={{0,6},{1,7},{2,4},{3,5},{4,2},{5,3},{6,0},{7,1},{8,14},{9,15},{10,... | collective-permute-start | bytes 12296 | tf_op jit(solution)/shard_map/ppermute | solution.py:652
  34.9 1.6 %collective-permute-done.5 = f32[8,128]{1,0:T(8,128)S(1)} collective-permute-done((f32[8,128]{1,0:T(8,128)S(1)}, f32[8,128]{1,0:T(8,128)S(1)}, u32[]{:S(2)}, u32[]{:S(2)}) %collective-permute-start.5) | collective-permute-done | bytes 4128 | tf_op jit(solution)/shard_map/ppermute | solution.py:652
  36.4 1.2 %shard_map.53 = f32[16,72,128]{2,1,0:T(8,128)} custom-call(f32[4,2,3,2,2,16,128]{6,5,4,3,2,1,0:T(8,128)S(1)} %get-tuple-element.31.rest, f32[8,128]{1,0:T(8,128)S(1)} %add.11.total_ref), custom_call_target="tpu_custom_call" | custom-call | tf_op jit(solution)/shard_map/pallas_call | solution.py:211
  37.7 0.1 all-to-all-done.own_ref
  37.8 5.0 %all-to-all-start.1 = ((f32[16,72,128]{2,1,0:T(8,128)}), f32[16,72,128]{2,1,0:T(8,128)S(1)}, u32[]{:S(2)}, u32[]{:S(2)}) async-start(f32[16,72,128]{2,1,0:T(8,128)} %shard_map.53), calls=%async_computation.1 | async-start | bytes 1179648 | tf_op jit(solution)/shard_map/all_to_all | solution.py:659
  42.8 0.0 copy-done
  42.8 0.6 %shard_map.54 = (f32[16,4,8,128]{3,2,1,0:T(8,128)S(1)}, f32[16,4,8,128]{3,2,1,0:T(8,128)S(1)}) custom-call(s32[2,9]{1,0:T(2,128)S(1)} %copy-done, f32[16,4,48,128]{3,2,1,0:T(8,128)S(1)} %all-to-all-done.own_ref), custom_call_target="tpu_custom_call" | custom-call | tf_op jit(solution)/shard_map/pallas_call | solution.py:575
  43.4 0.5 collective-permute-start.6
  43.8 0.7 %collective-permute-start.7 = (f32[16,4,8,128]{3,2,1,0:T(8,128)S(1)}, f32[16,4,8,128]{3,2,1,0:T(8,128)S(1)}, u32[]{:S(2)}, u32[]{:S(2)}) collective-permute-start(f32[16,4,8,128]{3,2,1,0:T(8,128)S(1)} %get-tuple-element.44), channel_id=1, source_target_pairs={{0,0},{7,7},{1,2},{2,1},{3,4},{4,3},{5,6},{6,5},{8,8},{15,15},{9,1... | collective-permute-start | bytes 786440 | tf_op jit(solution)/shard_map/ppermute | solution.py:681
  44.5 3.0 %shard_map.55.refs_4_ = f32[72,2,6,16,128]{4,3,2,1,0:T(8,128)} custom-call(s32[2,9]{1,0:T(2,128)S(1)} %copy-done, f32[16,4,48,128]{3,2,1,0:T(8,128)S(1)} %all-to-all-done.own_ref), custom_call_target="tpu_custom_call" | custom-call | tf_op jit(solution)/shard_map/pallas_call | solution.py:547
  47.5 0.0 collective-permute-done.6.refs_1_
  47.5 0.0 collective-permute-done.7.refs_2_
  47.5 6.2 %all-to-all-done.1.refs_3_ = f32[16,72,128]{2,1,0:T(8,128)S(1)} async-done(((f32[16,72,128]{2,1,0:T(8,128)}), f32[16,72,128]{2,1,0:T(8,128)S(1)}, u32[]{:S(2)}, u32[]{:S(2)}) %all-to-all-start.1) | async-done | bytes 589856 | tf_op jit(solution)/shard_map/all_to_all | solution.py:659
  53.7 2.1 %shard_map.56 = (f32[72,2,6,16,128]{4,3,2,1,0:T(8,128)}, f32[1,1]{1,0:T(1,128)}) custom-call(s32[2,9]{1,0:T(2,128)S(1)} %copy-done, f32[16,4,8,128]{3,2,1,0:T(8,128)S(1)} %collective-permute-done.6.refs_1_, f32[16,4,8,128]{3,2,1,0:T(8,128)S(1)} %collective-permute-done.7.refs_2_, ...), custom_call_target="tpu_custom_call", output_to_operand_aliasing={{0}: (4, {})} | custom-call | tf_op jit(solution)/shard_map/pallas_call | solution.py:635
  (3 shorter events, 0.0 us)
Async XLA Ops:
  2.9 8.4 %collective-permute-start.1 = (f32[2,8,8,128]{3,2,1,0:T(8,128)S(1)}, f32[2,8,8,128]{3,2,1,0:T(8,128)S(1)}, u32[]{:S(2)}, u32[]{:S(2)}) collective-permute-start(f32[2,8,8,128]{3,2,1,0:T(8,128)S(1)} %get-tuple-element.28), channel_id=1, source_target_pairs={{0,24},{8,0},{16,8},{24,16},{1,25},{9,1},{17,9},{25,17},{2,26},{10... | collective-permute-start | bytes 196616 | tf_op jit(solution)/shard_map/ppermute | solution.py:14
  5.9 5.5 %collective-permute-start = (f32[3,8,128]{2,1,0:T(8,128)S(1)}, f32[3,8,128]{2,1,0:T(8,128)S(1)}, u32[]{:S(2)}, u32[]{:S(2)}) collective-permute-start(f32[3,8,128]{2,1,0:T(8,128)S(1)} %get-tuple-element.27), channel_id=1, source_target_pairs={{0,96},{32,0},{64,32},{96,64},{1,97},{33,1},{65,33},{97,65},{2,98}... | collective-permute-start | bytes 36872 | tf_op jit(solution)/shard_map/ppermute | solution.py:14
  11.3 26.5 %all-to-all-start = ((f32[16,4,48,128]{3,2,1,0:T(8,128)}), f32[16,4,48,128]{3,2,1,0:T(8,128)S(1)}, u32[]{:S(2)}, u32[]{:S(2)}) async-start(f32[16,4,48,128]{3,2,1,0:T(8,128)} %shard_map.50), calls=%async_computation | async-start | bytes 3145728 | tf_op jit(solution)/shard_map/all_to_all | solution.py:659
  15.4 9.4 %collective-permute-start.2 = (f32[2,2,3,2,2,16,128]{6,5,4,3,2,1,0:T(8,128)S(1)}, f32[2,2,3,2,2,16,128]{6,5,4,3,2,1,0:T(8,128)S(1)}, u32[]{:S(2)}, u32[]{:S(2)}) collective-permute-start(f32[2,2,3,2,2,16,128]{6,5,4,3,2,1,0:T(8,128)S(1)} %get-tuple-element.40), channel_id=1, source_target_pairs={{0,7},{1,0},{2,1},{3,2},{4,3},{5,4},{6,5},{7,6},{8,15},{9,8},{10,9... | collective-permute-start | bytes 1179656 | tf_op jit(solution)/shard_map/ppermute | solution.py:14
  24.7 18.0 %copy-start = (s32[2,9]{1,0:T(2,128)S(1)}, s32[2,9]{1,0:T(2,128)}, u32[]{:S(2)}) copy-start(s32[2,9]{1,0:T(2,128)} %refs_0_.1) | copy-start | bytes 220
  26.6 1.2 %collective-permute-start.3 = (f32[8,128]{1,0:T(8,128)S(1)}, f32[8,128]{1,0:T(8,128)S(1)}, u32[]{:S(2)}, u32[]{:S(2)}) collective-permute-start(f32[8,128]{1,0:T(8,128)S(1)} %get-tuple-element.41), channel_id=1, source_target_pairs={{0,1},{1,0},{2,3},{3,2},{4,5},{5,4},{6,7},{7,6},{8,9},{9,8},{10,11... | collective-permute-start | bytes 12296 | tf_op jit(solution)/shard_map/ppermute | solution.py:652
  27.8 3.6 %collective-permute-start.4 = (f32[8,128]{1,0:T(8,128)S(1)}, f32[8,128]{1,0:T(8,128)S(1)}, u32[]{:S(2)}, u32[]{:S(2)}) collective-permute-start(f32[8,128]{1,0:T(8,128)S(1)} %add.9), channel_id=1, source_target_pairs={{0,2},{1,3},{2,0},{3,1},{4,6},{5,7},{6,4},{7,5},{8,10},{9,11},{10,... | collective-permute-start | bytes 12296 | tf_op jit(solution)/shard_map/ppermute | solution.py:652
  31.4 5.0 %collective-permute-start.5 = (f32[8,128]{1,0:T(8,128)S(1)}, f32[8,128]{1,0:T(8,128)S(1)}, u32[]{:S(2)}, u32[]{:S(2)}) collective-permute-start(f32[8,128]{1,0:T(8,128)S(1)} %add.10), channel_id=1, source_target_pairs={{0,6},{1,7},{2,4},{3,5},{4,2},{5,3},{6,0},{7,1},{8,14},{9,15},{10,... | collective-permute-start | bytes 12296 | tf_op jit(solution)/shard_map/ppermute | solution.py:652
  37.8 15.8 %all-to-all-start.1 = ((f32[16,72,128]{2,1,0:T(8,128)}), f32[16,72,128]{2,1,0:T(8,128)S(1)}, u32[]{:S(2)}, u32[]{:S(2)}) async-start(f32[16,72,128]{2,1,0:T(8,128)} %shard_map.53), calls=%async_computation.1 | async-start | bytes 1179648 | tf_op jit(solution)/shard_map/all_to_all | solution.py:659
  43.4 4.1 %collective-permute-start.6 = (f32[16,4,8,128]{3,2,1,0:T(8,128)S(1)}, f32[16,4,8,128]{3,2,1,0:T(8,128)S(1)}, u32[]{:S(2)}, u32[]{:S(2)}) collective-permute-start(f32[16,4,8,128]{3,2,1,0:T(8,128)S(1)} %get-tuple-element.43), channel_id=1, source_target_pairs={{0,1},{1,0},{2,3},{3,2},{4,5},{5,4},{6,7},{7,6},{8,9},{9,8},{10,11... | collective-permute-start | bytes 786440 | tf_op jit(solution)/shard_map/ppermute | solution.py:680
  43.8 3.6 %collective-permute-start.7 = (f32[16,4,8,128]{3,2,1,0:T(8,128)S(1)}, f32[16,4,8,128]{3,2,1,0:T(8,128)S(1)}, u32[]{:S(2)}, u32[]{:S(2)}) collective-permute-start(f32[16,4,8,128]{3,2,1,0:T(8,128)S(1)} %get-tuple-element.44), channel_id=1, source_target_pairs={{0,0},{7,7},{1,2},{2,1},{3,4},{4,3},{5,6},{6,5},{8,8},{15,15},{9,1... | collective-permute-start | bytes 786440 | tf_op jit(solution)/shard_map/ppermute | solution.py:681
where the time goes:
time: 56.1 us; the launch traced here: 55.8 us
  starting transfers between devices  23.8 us (42%)
  Pallas kernels  18.7 us (33%)
  waiting for transfers between devices  12.6 us (22%)
  between operations  0.76 us (1%)
    ppermute x3, starting transfers between devices, passed_along(): lax.ppermute(value, axis, [(i, (i + by) % count) for i in range(count)])  10 us
    all_to_all x2, starting transfers between devices, spread(): lax.all_to_all(payload, ('gx', 'gy', 'zt'), split_axis=0, concat_axis=0,...  9.04 us
    all_to_all x2, waiting for transfers between devices, spread(): lax.all_to_all(payload, ('gx', 'gy', 'zt'), split_axis=0, concat_axis=0,...  6.27 us
    ppermute x3, waiting for transfers between devices, summed(): lax.ppermute(value, axis, [(i, i ^ by) for i in range(count)])  6.22 us
    pallas_call x1, Pallas kernels, inner_plaquettes(): pl.pallas_call(inner_kernel, in_specs=[pl.BlockSpec(memory_space=pltpu.HB...  5.2 us
    ppermute x3, starting transfers between devices, summed(): lax.ppermute(value, axis, [(i, i ^ by) for i in range(count)])  3.6 us
    pallas_call x1, Pallas kernels, decoded(): pl.pallas_call(decode_kernel, in_specs=[pl.BlockSpec(memory_space=pl.ANY)...  2.95 us
    pallas_call x1, Pallas kernels, encoded(): pl.pallas_call(encode_kernel, in_specs=[pl.BlockSpec(memory_space=pltpu.V...  2.44 us
  transfers between devices with their start and end apart: 10, of which 6 were waited for; matrix products, arithmetic and copies ran while one was open for 0% of the time, Pallas kernels for 25%

commit v1 on v0

--- a/solution.py
+++ b/solution.py
@@ -141,34 +141,67 @@
     return pl.multiple_of(8 * (h ^ (lax.axis_index("zt") % 2)), 8)
 
 
-def encode_kernel(taken, out_ref, given, out_sem):
+def copies_in(links_ref, m, taken, rest, sem, n):
+    rows = pl.ds(0, 2)
+    sources = [links_ref.at[m, rows, :, :, t, pl.ds(0, 2)] for t in range(2)] + [links_ref.at[m, rows, :, :, :, 3]]
+    copies = [pltpu.make_async_copy(x, taken.at[3 * n + i], sem.at[n, i]) for i, x in enumerate(sources)]
+    return copies + [pltpu.make_async_copy(links_ref.at[m, rows, :, :, :, 2], rest.at[n], sem.at[n, 3])]
+
+
+def encode_kernel(links_ref, taken, out_ref, z_ref, rest_3, taken_3, given, in_sem, z_sem, out_sem):
+    copies = copies_in(links_ref, 3, taken_3, rest_3, in_sem, 0)
+    copies += [pltpu.make_async_copy(links_ref.at[pl.ds(0, 2), pl.ds(0, 2), :, :, :, 0], z_ref, z_sem)]
+    for copy in copies:
+        copy.start()
+
     def copy_out(step, h):
         at = pl.ds(pl.multiple_of((step % 3) * 16, 16), 16)
         return pltpu.make_async_copy(
             given.at[step, pl.ds(8 * h, 8)], out_ref.at[pl.ds(block_half(h), 8), step // 3, at], out_sem.at[h, step]
         )
 
-    def one(step, carry):
-        encode_planes(taken.at[step].reshape(12 * 32, 128), given.at[step].reshape(16 * 16, 128), 16)
+    def one(source, step):
+        encode_planes(source.reshape(12 * 32, 128), given.at[step].reshape(16 * 16, 128), 16)
         copy_out(step, 0).start()
         copy_out(step, 1).start()
+
+    def first(step, carry):
+        one(taken.at[step], step)
         return carry
 
-    lax.fori_loop(0, 12, one, 0)
+    def second(pair, carry):
+        one(taken_3.at[pair], 9 + pair)
+        return carry
+
+    lax.fori_loop(0, 9, first, 0)
+    for copy in copies:
+        copy.wait()
+    lax.fori_loop(0, 3, second, 0)
     for step in range(12):
         copy_out(step, 0).wait()
         copy_out(step, 1).wait()
 
 
-def encoded(taken):
+def encoded(links, taken):
+    kept = pl.BlockSpec(memory_space=pltpu.VMEM)
     return pl.pallas_call(
         encode_kernel,
-        in_specs=[pl.BlockSpec(memory_space=pltpu.VMEM)],
-        out_specs=pl.BlockSpec(memory_space=pltpu.HBM),
-        out_shape=pltpu.HBM((16, 4, 48, 128), jnp.float32),
-        scratch_shapes=[pltpu.VMEM((12, 16, 16, 128), jnp.float32), pltpu.SemaphoreType.DMA((2, 12))],
+        in_specs=[pl.BlockSpec(memory_space=pltpu.HBM), kept],
+        out_specs=[pl.BlockSpec(memory_space=pltpu.HBM), kept, kept],
+        out_shape=[
+            pltpu.HBM((16, 4, 48, 128), jnp.float32),
+            pltpu.VMEM((2, 2, 3, 2, 2, 16, 128), jnp.float32),
+            pltpu.VMEM((1, 2, 3, 2, 2, 16, 128), jnp.float32),
+        ],
+        scratch_shapes=[
+            pltpu.VMEM((3, 2, 3, 2, 2, 16, 128), jnp.float32),
+            pltpu.VMEM((12, 16, 16, 128), jnp.float32),
+            pltpu.SemaphoreType.DMA((1, 4)),
+            pltpu.SemaphoreType.DMA,
+            pltpu.SemaphoreType.DMA((2, 12)),
+        ],
         compiler_params=pltpu.CompilerParams(vmem_limit_bytes=VMEM_LIMIT),
-    )(taken)
+    )(links, taken)
 
 
 class ShiftedRows:
@@ -180,7 +213,7 @@
         self.ref[pl.ds(self.by + at[0].start, at[0].size, stride=at[0].stride), :] = value
 
 
-def encode_rest_kernel(rest, total_ref, out_ref, given, out_sem):
+def encode_rest_kernel(rest, rest_3, total_ref, out_ref, given, out_sem):
     out = given.reshape(16 * 72, 128)
     for n in range(16):
         given[n, pl.ds(64, 8), :] = total_ref[...]
@@ -194,50 +227,40 @@
     copy_out(4, 8, 0).start()
     copy_out(4, 8, 1).start()
 
-    def one(m, carry):
-        encode_planes(rest.at[m].reshape(12 * 32, 128), ShiftedRows(out, m * 16), 72)
+    def one(source, m):
+        encode_planes(source.reshape(12 * 32, 128), ShiftedRows(out, m * 16), 72)
         copy_out(m, 16, 0).start()
         copy_out(m, 16, 1).start()
+
+    def first(m, carry):
+        one(rest.at[m], m)
         return carry
 
-    lax.fori_loop(0, 4, one, 0)
+    lax.fori_loop(0, 3, first, 0)
+    one(rest_3.at[0], 3)
     for h in range(2):
         for m in range(4):
             copy_out(m, 16, h).wait()
         copy_out(4, 8, h).wait()
 
 
-def encoded_rest(rest, total):
+def encoded_rest(rest, rest_3, total):
     return pl.pallas_call(
         encode_rest_kernel,
-        in_specs=[pl.BlockSpec(memory_space=pltpu.VMEM)] * 2,
+        in_specs=[pl.BlockSpec(memory_space=pltpu.VMEM)] * 3,
         out_specs=pl.BlockSpec(memory_space=pltpu.HBM),
         out_shape=pltpu.HBM((16, 72, 128), jnp.float32),
         scratch_shapes=[pltpu.VMEM((16, 72, 128), jnp.float32), pltpu.SemaphoreType.DMA((2, 5))],
         compiler_params=pltpu.CompilerParams(vmem_limit_bytes=VMEM_LIMIT),
-    )(rest, total)
-
-
-def take_kernel(links_ref, x_ref, y_ref, z_ref, taken, rest, in_sem, rest_sem, z_sem):
-    def copy_in(m, pair):
-        if pair == 2:
-            source = links_ref.at[m, pl.ds(0, 2), :, :, :, 3]
-        else:
-            source = links_ref.at[m, pl.ds(0, 2), :, :, pair, pl.ds(0, 2)]
-        return pltpu.make_async_copy(source, taken.at[3 * m + pair], in_sem.at[3 * m + pair])
-
-    def copy_rest(m):
-        return pltpu.make_async_copy(links_ref.at[m, pl.ds(0, 2), :, :, :, 2], rest.at[m], rest_sem.at[m])
-
-    def copies(m):
-        return [copy_in(m, pair) for pair in range(3)] + [copy_rest(m)]
-
-    copy_z = pltpu.make_async_copy(links_ref.at[pl.ds(0, 2), pl.ds(0, 2), :, :, :, 0], z_ref, z_sem)
-    order = (2, 1, 0, 3)
+    )(rest, rest_3, total)
+
+
+def take_kernel(links_ref, x_ref, y_ref, taken, rest, in_sem):
+    order = (2, 1, 0)
+    copies = {m: copies_in(links_ref, m, taken, rest, in_sem, m) for m in order}
     for m in order:
-        for copy in copies(m):
+        for copy in copies[m]:
             copy.start()
-    copy_z.start()
 
     def rows(m, r, c, i, k, start, size):
         t, z = k // 4, k % 4
@@ -267,7 +290,7 @@
                     got[n // 8] = value if got[n // 8] is None else jnp.where(lane == at, value, got[n // 8])
 
     for m in order:
-        for copy in copies(m):
+        for copy in copies[m]:
             copy.wait()
         if m in (1, 2):
             column_face(m)
@@ -275,7 +298,6 @@
             row_face(m)
     for n in range(3):
         x_ref[n] = got[n]
-    copy_z.wait()
 
 
 def taken_links(links):
@@ -283,19 +305,14 @@
     return pl.pallas_call(
         take_kernel,
         in_specs=[pl.BlockSpec(memory_space=pltpu.HBM)],
-        out_specs=[kept] * 5,
+        out_specs=[kept] * 4,
         out_shape=[
             pltpu.VMEM((3, 8, 128), jnp.float32),
             pltpu.VMEM((2, 8, 8, 128), jnp.float32),
-            pltpu.VMEM((2, 2, 3, 2, 2, 16, 128), jnp.float32),
-            pltpu.VMEM((12, 2, 3, 2, 2, 16, 128), jnp.float32),
-            pltpu.VMEM((4, 2, 3, 2, 2, 16, 128), jnp.float32),
+            pltpu.VMEM((9, 2, 3, 2, 2, 16, 128), jnp.float32),
+            pltpu.VMEM((3, 2, 3, 2, 2, 16, 128), jnp.float32),
         ],
-        scratch_shapes=[
-            pltpu.SemaphoreType.DMA((12,)),
-            pltpu.SemaphoreType.DMA((4,)),
-            pltpu.SemaphoreType.DMA,
-        ],
+        scratch_shapes=[pltpu.SemaphoreType.DMA((3, 4))],
         compiler_params=pltpu.CompilerParams(vmem_limit_bytes=VMEM_LIMIT),
     )(links)
 
@@ -663,17 +680,17 @@
 
 def local(links, bounds):
     held = pltpu.with_memory_space_constraint(links, pltpu.HBM)
-    x_face, y_face, z_face, taken, rest = taken_links(held)
+    x_face, y_face, taken, rest = taken_links(held)
     y_face = passed_along(y_face, "gy", -1)
     x_face = passed_along(x_face, "gx", -1)
-    payload = encoded(taken)
+    payload, z_face, rest_3 = encoded(held, taken)
     payload, links, x_face, y_face, z_face = lax.optimization_barrier((payload, links, x_face, y_face, z_face))
     held = pltpu.with_memory_space_constraint(links, pltpu.HBM)
     moved = spread(payload)
     z_face = passed_along(z_face, "zt", -1)
     plaquette, total = outer_plaquettes(*inner_plaquettes(held, x_face, y_face), z_face)
     total = summed(total, (("zt", 1), ("zt", 2), ("zt", 6)))
-    rest = encoded_rest(rest, total)
+    rest = encoded_rest(rest, rest_3, total)
     moved, rest = lax.optimization_barrier((moved, rest))
     moved_rest = spread(rest)
     first, second = cut_planes(bounds, moved)

time: 56.1 us -> 55.8 us (level)
  transfers between devices with their start and end apart: 10 -> 10, of which waited for: 6 -> 6; matrix products, arithmetic and copies ran while one was open for 0% -> 0% of each run, Pallas kernels for 25% -> 26%
where the time goes in v1:
time: 55.8 us; the launch traced here: 55.4 us
  starting transfers between devices  23.4 us (42%)
  Pallas kernels  18.7 us (34%)
  waiting for transfers between devices  12.5 us (22%)
  between operations  0.76 us (1%)
    ppermute x3, starting transfers between devices, passed_along(): lax.ppermute(value, axis, [(i, (i + by) % count) for i in range(count)])  9.98 us
    all_to_all x2, starting transfers between devices, spread(): lax.all_to_all(payload, ('gx', 'gy', 'zt'), split_axis=0, concat_axis=0,...  8.7 us
    all_to_all x2, waiting for transfers between devices, spread(): lax.all_to_all(payload, ('gx', 'gy', 'zt'), split_axis=0, concat_axis=0,...  6.23 us
    ppermute x3, waiting for transfers between devices, summed(): lax.ppermute(value, axis, [(i, i ^ by) for i in range(count)])  6.22 us
    pallas_call x1, Pallas kernels, inner_plaquettes(): pl.pallas_call(inner_kernel, in_specs=[pl.BlockSpec(memory_space=pltpu.HB...  5.2 us
    ppermute x3, starting transfers between devices, summed(): lax.ppermute(value, axis, [(i, i ^ by) for i in range(count)])  3.6 us
    pallas_call x1, Pallas kernels, decoded(): pl.pallas_call(decode_kernel, in_specs=[pl.BlockSpec(memory_space=pl.ANY)...  2.95 us
    pallas_call x1, Pallas kernels, encoded(): pl.pallas_call(encode_kernel, in_specs=[pl.BlockSpec(memory_space=pltpu.H...  2.84 us
  transfers between devices with their start and end apart: 10, of which 6 were waited for; matrix products, arithmetic and copies ran while one was open for 0% of the time, Pallas kernels for 26%

profile of v1, /device:TPU:0, one launch (start us, length us, event | category | flops | bytes accessed | tf_op | source)
XLA Modules:
  0.0 55.4 jit_solution(7617803978055785970)
XLA Ops:
  0.6 2.0 %shard_map.49 = (f32[3,8,128]{2,1,0:T(8,128)S(1)}, f32[2,8,8,128]{3,2,1,0:T(8,128)S(1)}, f32[9,2,3,2,2,16,128]{6,5,4,3,2,1,0:T(8,128)S(1)}, f32[3,2,3,2,2,16,128]{6,5,4,3,2,1,0:T(8,128)S(1)}) custom-call(f32[4,3,3,2,2,4,16,128]{7,6,5,4,3,2,1,0:T(8,128)} %links_ref.4), custom_call_target="tpu_custom_call" | custom-call | tf_op jit(solution)/shard_map/pallas_call | solution.py:305
  2.6 2.9 %collective-permute-start.1 = (f32[2,8,8,128]{3,2,1,0:T(8,128)S(1)}, f32[2,8,8,128]{3,2,1,0:T(8,128)S(1)}, u32[]{:S(2)}, u32[]{:S(2)}) collective-permute-start(f32[2,8,8,128]{3,2,1,0:T(8,128)S(1)} %get-tuple-element.31), channel_id=1, source_target_pairs={{0,24},{8,0},{16,8},{24,16},{1,25},{9,1},{17,9},{25,17},{2,26},{10... | collective-permute-start | bytes 196616 | tf_op jit(solution)/shard_map/ppermute | solution.py:14
  5.5 3.0 %collective-permute-start = (f32[3,8,128]{2,1,0:T(8,128)S(1)}, f32[3,8,128]{2,1,0:T(8,128)S(1)}, u32[]{:S(2)}, u32[]{:S(2)}) collective-permute-start(f32[3,8,128]{2,1,0:T(8,128)S(1)} %get-tuple-element.30), channel_id=1, source_target_pairs={{0,96},{32,0},{64,32},{96,64},{1,97},{33,1},{65,33},{97,65},{2,98}... | collective-permute-start | bytes 36872 | tf_op jit(solution)/shard_map/ppermute | solution.py:14
  8.5 2.8 %shard_map.50 = (f32[16,4,48,128]{3,2,1,0:T(8,128)}, f32[2,2,3,2,2,16,128]{6,5,4,3,2,1,0:T(8,128)S(1)}, f32[1,2,3,2,2,16,128]{6,5,4,3,2,1,0:T(8,128)S(1)}) custom-call(f32[4,3,3,2,2,4,16,128]{7,6,5,4,3,2,1,0:T(8,128)} %links_ref.4, f32[9,2,3,2,2,16,128]{6,5,4,3,2,1,0:T(8,128)S(1)} %get-tuple-element.28.taken), custom_call_target="tpu_custom_call" | custom-call | tf_op jit(solution)/shard_map/pallas_call | solution.py:187
  11.4 0.0 collective-permute-done.x_ref
  11.4 0.0 collective-permute-done.1.y_ref
  11.4 3.7 %all-to-all-start = ((f32[16,4,48,128]{3,2,1,0:T(8,128)}), f32[16,4,48,128]{3,2,1,0:T(8,128)S(1)}, u32[]{:S(2)}, u32[]{:S(2)}) async-start(f32[16,4,48,128]{3,2,1,0:T(8,128)} %get-tuple-element.33), calls=%async_computation | async-start | bytes 3145728 | tf_op jit(solution)/shard_map/all_to_all | solution.py:676
  15.1 4.1 %collective-permute-start.2 = (f32[2,2,3,2,2,16,128]{6,5,4,3,2,1,0:T(8,128)S(1)}, f32[2,2,3,2,2,16,128]{6,5,4,3,2,1,0:T(8,128)S(1)}, u32[]{:S(2)}, u32[]{:S(2)}) collective-permute-start(f32[2,2,3,2,2,16,128]{6,5,4,3,2,1,0:T(8,128)S(1)} %get-tuple-element.44), channel_id=1, source_target_pairs={{0,7},{1,0},{2,1},{3,2},{4,3},{5,4},{6,5},{7,6},{8,15},{9,8},{10,9... | collective-permute-start | bytes 1179656 | tf_op jit(solution)/shard_map/ppermute | solution.py:14
  19.2 5.2 %shard_map.51 = (f32[2,4,16,128]{3,2,1,0:T(8,128)S(1)}, f32[8,128]{1,0:T(8,128)S(1)}, f32[3,18,2,4,16,128]{5,4,3,2,1,0:T(8,128)S(1)}, f32[2,18,8,128]{3,2,1,0:T(8,128)S(1)}, f32[2,18,8,128]{3,2,1,0:T(8,128)S(1)}) custom-call(f32[4,3,3,2,2,4,16,128]{7,6,5,4,3,2,1,0:T(8,128)} %links_ref.4, f32[3,8,128]{2,1,0:T(8,128)S(1)} %collective-permute-done.x_ref, ...), custom_call_target="tpu_custom_call" | custom-call | tf_op jit(solution)/shard_map/pallas_call | solution.py:437
  24.4 0.0 copy-start
  24.4 0.1 collective-permute-done.2.z_ref
  24.5 1.8 %shard_map.52 = (f32[2,4,16,128]{3,2,1,0:T(8,128)}, f32[8,128]{1,0:T(8,128)S(1)}) custom-call(f32[2,4,16,128]{3,2,1,0:T(8,128)S(1)} %get-tuple-element.39.inner_ref, f32[8,128]{1,0:T(8,128)S(1)} %get-tuple-element.40.part_ref, f32[3,18,2,4,16,128]{5,4,3,2,1,0:T(8,128)S(1)} %get-tuple-element.41.unit, f32[2,18,8,128]{3,2,1,0:T(8,128)S(1)} %get-tuple-element.42.x_edge, ...), custom_call_target="tpu_custom_call" | custom-call | tf_op jit(solution)/shard_map/pallas_call | solution.py:479
  26.2 0.0 collective-permute-start.3
  26.3 1.2 %collective-permute-done.3 = f32[8,128]{1,0:T(8,128)S(1)} collective-permute-done((f32[8,128]{1,0:T(8,128)S(1)}, f32[8,128]{1,0:T(8,128)S(1)}, u32[]{:S(2)}, u32[]{:S(2)}) %collective-permute-start.3) | collective-permute-done | bytes 4128 | tf_op jit(solution)/shard_map/ppermute | solution.py:669
  27.4 0.1 collective-permute-start.4
  27.6 3.5 %collective-permute-done.4 = f32[8,128]{1,0:T(8,128)S(1)} collective-permute-done((f32[8,128]{1,0:T(8,128)S(1)}, f32[8,128]{1,0:T(8,128)S(1)}, u32[]{:S(2)}, u32[]{:S(2)}) %collective-permute-start.4) | collective-permute-done | bytes 4128 | tf_op jit(solution)/shard_map/ppermute | solution.py:669
  31.0 3.5 %collective-permute-start.5 = (f32[8,128]{1,0:T(8,128)S(1)}, f32[8,128]{1,0:T(8,128)S(1)}, u32[]{:S(2)}, u32[]{:S(2)}) collective-permute-start(f32[8,128]{1,0:T(8,128)S(1)} %add.10), channel_id=1, source_target_pairs={{0,6},{1,7},{2,4},{3,5},{4,2},{5,3},{6,0},{7,1},{8,14},{9,15},{10,... | collective-permute-start | bytes 12296 | tf_op jit(solution)/shard_map/ppermute | solution.py:669
  34.5 1.6 %collective-permute-done.5 = f32[8,128]{1,0:T(8,128)S(1)} collective-permute-done((f32[8,128]{1,0:T(8,128)S(1)}, f32[8,128]{1,0:T(8,128)S(1)}, u32[]{:S(2)}, u32[]{:S(2)}) %collective-permute-start.5) | collective-permute-done | bytes 4128 | tf_op jit(solution)/shard_map/ppermute | solution.py:669
  36.1 1.3 %shard_map.53 = f32[16,72,128]{2,1,0:T(8,128)} custom-call(f32[3,2,3,2,2,16,128]{6,5,4,3,2,1,0:T(8,128)S(1)} %get-tuple-element.34.rest, f32[1,2,3,2,2,16,128]{6,5,4,3,2,1,0:T(8,128)S(1)} %get-tuple-element.35.rest_3, f32[8,128]{1,0:T(8,128)S(1)} %add.11.total_ref), custom_call_target="tpu_custom_call" | custom-call | tf_op jit(solution)/shard_map/pallas_call | solution.py:248
  37.4 0.1 all-to-all-done.own_ref
  37.5 5.0 %all-to-all-start.1 = ((f32[16,72,128]{2,1,0:T(8,128)}), f32[16,72,128]{2,1,0:T(8,128)S(1)}, u32[]{:S(2)}, u32[]{:S(2)}) async-start(f32[16,72,128]{2,1,0:T(8,128)} %shard_map.53), calls=%async_computation.1 | async-start | bytes 1179648 | tf_op jit(solution)/shard_map/all_to_all | solution.py:676
  42.4 0.0 copy-done
  42.5 0.6 %shard_map.54 = (f32[16,4,8,128]{3,2,1,0:T(8,128)S(1)}, f32[16,4,8,128]{3,2,1,0:T(8,128)S(1)}) custom-call(s32[2,9]{1,0:T(2,128)S(1)} %copy-done, f32[16,4,48,128]{3,2,1,0:T(8,128)S(1)} %all-to-all-done.own_ref), custom_call_target="tpu_custom_call" | custom-call | tf_op jit(solution)/shard_map/pallas_call | solution.py:592
  43.1 0.5 collective-permute-start.6
  43.5 0.7 %collective-permute-start.7 = (f32[16,4,8,128]{3,2,1,0:T(8,128)S(1)}, f32[16,4,8,128]{3,2,1,0:T(8,128)S(1)}, u32[]{:S(2)}, u32[]{:S(2)}) collective-permute-start(f32[16,4,8,128]{3,2,1,0:T(8,128)S(1)} %get-tuple-element.48), channel_id=1, source_target_pairs={{0,0},{7,7},{1,2},{2,1},{3,4},{4,3},{5,6},{6,5},{8,8},{15,15},{9,1... | collective-permute-start | bytes 786440 | tf_op jit(solution)/shard_map/ppermute | solution.py:698
  44.2 3.0 %shard_map.55.refs_4_ = f32[72,2,6,16,128]{4,3,2,1,0:T(8,128)} custom-call(s32[2,9]{1,0:T(2,128)S(1)} %copy-done, f32[16,4,48,128]{3,2,1,0:T(8,128)S(1)} %all-to-all-done.own_ref), custom_call_target="tpu_custom_call" | custom-call | tf_op jit(solution)/shard_map/pallas_call | solution.py:564
  47.1 0.0 collective-permute-done.6.refs_1_
  47.2 0.0 collective-permute-done.7.refs_2_
  47.2 6.1 %all-to-all-done.1.refs_3_ = f32[16,72,128]{2,1,0:T(8,128)S(1)} async-done(((f32[16,72,128]{2,1,0:T(8,128)}), f32[16,72,128]{2,1,0:T(8,128)S(1)}, u32[]{:S(2)}, u32[]{:S(2)}) %all-to-all-start.1) | async-done | bytes 589856 | tf_op jit(solution)/shard_map/all_to_all | solution.py:676
  53.3 2.1 %shard_map.56 = (f32[72,2,6,16,128]{4,3,2,1,0:T(8,128)}, f32[1,1]{1,0:T(1,128)}) custom-call(s32[2,9]{1,0:T(2,128)S(1)} %copy-done, f32[16,4,8,128]{3,2,1,0:T(8,128)S(1)} %collective-permute-done.6.refs_1_, f32[16,4,8,128]{3,2,1,0:T(8,128)S(1)} %collective-permute-done.7.refs_2_, ...), custom_call_target="tpu_custom_call", output_to_operand_aliasing={{0}: (4, {})} | custom-call | tf_op jit(solution)/shard_map/pallas_call | solution.py:652
  (3 shorter events, 0.0 us)
Async XLA Ops:
  2.6 8.8 %collective-permute-start.1 = (f32[2,8,8,128]{3,2,1,0:T(8,128)S(1)}, f32[2,8,8,128]{3,2,1,0:T(8,128)S(1)}, u32[]{:S(2)}, u32[]{:S(2)}) collective-permute-start(f32[2,8,8,128]{3,2,1,0:T(8,128)S(1)} %get-tuple-element.31), channel_id=1, source_target_pairs={{0,24},{8,0},{16,8},{24,16},{1,25},{9,1},{17,9},{25,17},{2,26},{10... | collective-permute-start | bytes 196616 | tf_op jit(solution)/shard_map/ppermute | solution.py:14
  5.5 5.9 %collective-permute-start = (f32[3,8,128]{2,1,0:T(8,128)S(1)}, f32[3,8,128]{2,1,0:T(8,128)S(1)}, u32[]{:S(2)}, u32[]{:S(2)}) collective-permute-start(f32[3,8,128]{2,1,0:T(8,128)S(1)} %get-tuple-element.30), channel_id=1, source_target_pairs={{0,96},{32,0},{64,32},{96,64},{1,97},{33,1},{65,33},{97,65},{2,98}... | collective-permute-start | bytes 36872 | tf_op jit(solution)/shard_map/ppermute | solution.py:14
  11.4 26.1 %all-to-all-start = ((f32[16,4,48,128]{3,2,1,0:T(8,128)}), f32[16,4,48,128]{3,2,1,0:T(8,128)S(1)}, u32[]{:S(2)}, u32[]{:S(2)}) async-start(f32[16,4,48,128]{3,2,1,0:T(8,128)} %get-tuple-element.33), calls=%async_computation | async-start | bytes 3145728 | tf_op jit(solution)/shard_map/all_to_all | solution.py:676
  15.1 9.4 %collective-permute-start.2 = (f32[2,2,3,2,2,16,128]{6,5,4,3,2,1,0:T(8,128)S(1)}, f32[2,2,3,2,2,16,128]{6,5,4,3,2,1,0:T(8,128)S(1)}, u32[]{:S(2)}, u32[]{:S(2)}) collective-permute-start(f32[2,2,3,2,2,16,128]{6,5,4,3,2,1,0:T(8,128)S(1)} %get-tuple-element.44), channel_id=1, source_target_pairs={{0,7},{1,0},{2,1},{3,2},{4,3},{5,4},{6,5},{7,6},{8,15},{9,8},{10,9... | collective-permute-start | bytes 1179656 | tf_op jit(solution)/shard_map/ppermute | solution.py:14
  24.4 18.1 %copy-start = (s32[2,9]{1,0:T(2,128)S(1)}, s32[2,9]{1,0:T(2,128)}, u32[]{:S(2)}) copy-start(s32[2,9]{1,0:T(2,128)} %refs_0_.1) | copy-start | bytes 220
  26.2 1.2 %collective-permute-start.3 = (f32[8,128]{1,0:T(8,128)S(1)}, f32[8,128]{1,0:T(8,128)S(1)}, u32[]{:S(2)}, u32[]{:S(2)}) collective-permute-start(f32[8,128]{1,0:T(8,128)S(1)} %get-tuple-element.45), channel_id=1, source_target_pairs={{0,1},{1,0},{2,3},{3,2},{4,5},{5,4},{6,7},{7,6},{8,9},{9,8},{10,11... | collective-permute-start | bytes 12296 | tf_op jit(solution)/shard_map/ppermute | solution.py:669
  27.4 3.6 %collective-permute-start.4 = (f32[8,128]{1,0:T(8,128)S(1)}, f32[8,128]{1,0:T(8,128)S(1)}, u32[]{:S(2)}, u32[]{:S(2)}) collective-permute-start(f32[8,128]{1,0:T(8,128)S(1)} %add.9), channel_id=1, source_target_pairs={{0,2},{1,3},{2,0},{3,1},{4,6},{5,7},{6,4},{7,5},{8,10},{9,11},{10,... | collective-permute-start | bytes 12296 | tf_op jit(solution)/shard_map/ppermute | solution.py:669
  31.0 5.0 %collective-permute-start.5 = (f32[8,128]{1,0:T(8,128)S(1)}, f32[8,128]{1,0:T(8,128)S(1)}, u32[]{:S(2)}, u32[]{:S(2)}) collective-permute-start(f32[8,128]{1,0:T(8,128)S(1)} %add.10), channel_id=1, source_target_pairs={{0,6},{1,7},{2,4},{3,5},{4,2},{5,3},{6,0},{7,1},{8,14},{9,15},{10,... | collective-permute-start | bytes 12296 | tf_op jit(solution)/shard_map/ppermute | solution.py:669
  37.5 15.9 %all-to-all-start.1 = ((f32[16,72,128]{2,1,0:T(8,128)}), f32[16,72,128]{2,1,0:T(8,128)S(1)}, u32[]{:S(2)}, u32[]{:S(2)}) async-start(f32[16,72,128]{2,1,0:T(8,128)} %shard_map.53), calls=%async_computation.1 | async-start | bytes 1179648 | tf_op jit(solution)/shard_map/all_to_all | solution.py:676
  43.1 4.1 %collective-permute-start.6 = (f32[16,4,8,128]{3,2,1,0:T(8,128)S(1)}, f32[16,4,8,128]{3,2,1,0:T(8,128)S(1)}, u32[]{:S(2)}, u32[]{:S(2)}) collective-permute-start(f32[16,4,8,128]{3,2,1,0:T(8,128)S(1)} %get-tuple-element.47), channel_id=1, source_target_pairs={{0,1},{1,0},{2,3},{3,2},{4,5},{5,4},{6,7},{7,6},{8,9},{9,8},{10,11... | collective-permute-start | bytes 786440 | tf_op jit(solution)/shard_map/ppermute | solution.py:697
  43.5 3.6 %collective-permute-start.7 = (f32[16,4,8,128]{3,2,1,0:T(8,128)S(1)}, f32[16,4,8,128]{3,2,1,0:T(8,128)S(1)}, u32[]{:S(2)}, u32[]{:S(2)}) collective-permute-start(f32[16,4,8,128]{3,2,1,0:T(8,128)S(1)} %get-tuple-element.48), channel_id=1, source_target_pairs={{0,0},{7,7},{1,2},{2,1},{3,4},{4,3},{5,6},{6,5},{8,8},{15,15},{9,1... | collective-permute-start | bytes 786440 | tf_op jit(solution)/shard_map/ppermute | solution.py:698

commit v2 on v1

--- a/solution.py
+++ b/solution.py
@@ -689,7 +689,7 @@
     moved = spread(payload)
     z_face = passed_along(z_face, "zt", -1)
     plaquette, total = outer_plaquettes(*inner_plaquettes(held, x_face, y_face), z_face)
-    total = summed(total, (("zt", 1), ("zt", 2), ("zt", 6)))
+    total = summed(total, (("zt", 1), ("zt", 6), ("zt", 2)))
     rest = encoded_rest(rest, rest_3, total)
     moved, rest = lax.optimization_barrier((moved, rest))
     moved_rest = spread(rest)

time: 55.8 us -> 55.9 us (level)
  no operation moved by 1% of the time
where the time goes in v2:
time: 55.9 us; the launch traced here: 55.6 us
  starting transfers between devices  23.4 us (42%)
  Pallas kernels  18.7 us (33%)
  waiting for transfers between devices  12.7 us (23%)
  between operations  0.76 us (1%)
    ppermute x3, starting transfers between devices, passed_along(): lax.ppermute(value, axis, [(i, (i + by) % count) for i in range(count)])  9.98 us
    all_to_all x2, starting transfers between devices, spread(): lax.all_to_all(payload, ('gx', 'gy', 'zt'), split_axis=0, concat_axis=0,...  8.7 us
    ppermute x3, waiting for transfers between devices, summed(): lax.ppermute(value, axis, [(i, i ^ by) for i in range(count)])  6.35 us
    all_to_all x2, waiting for transfers between devices, spread(): lax.all_to_all(payload, ('gx', 'gy', 'zt'), split_axis=0, concat_axis=0,...  6.26 us
    pallas_call x1, Pallas kernels, inner_plaquettes(): pl.pallas_call(inner_kernel, in_specs=[pl.BlockSpec(memory_space=pltpu.HB...  5.2 us
    ppermute x3, starting transfers between devices, summed(): lax.ppermute(value, axis, [(i, i ^ by) for i in range(count)])  3.47 us
    pallas_call x1, Pallas kernels, decoded(): pl.pallas_call(decode_kernel, in_specs=[pl.BlockSpec(memory_space=pl.ANY)...  2.95 us
    pallas_call x1, Pallas kernels, encoded(): pl.pallas_call(encode_kernel, in_specs=[pl.BlockSpec(memory_space=pltpu.H...  2.84 us
  transfers between devices with their start and end apart: 10, of which 6 were waited for; matrix products, arithmetic and copies ran while one was open for 0% of the time, Pallas kernels for 26%

profile of v2, /device:TPU:0, one launch (start us, length us, event | category | flops | bytes accessed | tf_op | source)
XLA Modules:
  0.0 55.6 jit_solution(18402530340555379184)
XLA Ops:
  0.6 2.0 %shard_map.49 = (f32[3,8,128]{2,1,0:T(8,128)S(1)}, f32[2,8,8,128]{3,2,1,0:T(8,128)S(1)}, f32[9,2,3,2,2,16,128]{6,5,4,3,2,1,0:T(8,128)S(1)}, f32[3,2,3,2,2,16,128]{6,5,4,3,2,1,0:T(8,128)S(1)}) custom-call(f32[4,3,3,2,2,4,16,128]{7,6,5,4,3,2,1,0:T(8,128)} %links_ref.4), custom_call_target="tpu_custom_call" | custom-call | tf_op jit(solution)/shard_map/pallas_call | solution.py:305
  2.6 2.9 %collective-permute-start.1 = (f32[2,8,8,128]{3,2,1,0:T(8,128)S(1)}, f32[2,8,8,128]{3,2,1,0:T(8,128)S(1)}, u32[]{:S(2)}, u32[]{:S(2)}) collective-permute-start(f32[2,8,8,128]{3,2,1,0:T(8,128)S(1)} %get-tuple-element.31), channel_id=1, source_target_pairs={{0,24},{8,0},{16,8},{24,16},{1,25},{9,1},{17,9},{25,17},{2,26},{10... | collective-permute-start | bytes 196616 | tf_op jit(solution)/shard_map/ppermute | solution.py:14
  5.5 3.0 %collective-permute-start = (f32[3,8,128]{2,1,0:T(8,128)S(1)}, f32[3,8,128]{2,1,0:T(8,128)S(1)}, u32[]{:S(2)}, u32[]{:S(2)}) collective-permute-start(f32[3,8,128]{2,1,0:T(8,128)S(1)} %get-tuple-element.30), channel_id=1, source_target_pairs={{0,96},{32,0},{64,32},{96,64},{1,97},{33,1},{65,33},{97,65},{2,98}... | collective-permute-start | bytes 36872 | tf_op jit(solution)/shard_map/ppermute | solution.py:14
  8.5 2.8 %shard_map.50 = (f32[16,4,48,128]{3,2,1,0:T(8,128)}, f32[2,2,3,2,2,16,128]{6,5,4,3,2,1,0:T(8,128)S(1)}, f32[1,2,3,2,2,16,128]{6,5,4,3,2,1,0:T(8,128)S(1)}) custom-call(f32[4,3,3,2,2,4,16,128]{7,6,5,4,3,2,1,0:T(8,128)} %links_ref.4, f32[9,2,3,2,2,16,128]{6,5,4,3,2,1,0:T(8,128)S(1)} %get-tuple-element.28.taken), custom_call_target="tpu_custom_call" | custom-call | tf_op jit(solution)/shard_map/pallas_call | solution.py:187
  11.4 0.0 collective-permute-done.x_ref
  11.4 0.0 collective-permute-done.1.y_ref
  11.4 3.7 %all-to-all-start = ((f32[16,4,48,128]{3,2,1,0:T(8,128)}), f32[16,4,48,128]{3,2,1,0:T(8,128)S(1)}, u32[]{:S(2)}, u32[]{:S(2)}) async-start(f32[16,4,48,128]{3,2,1,0:T(8,128)} %get-tuple-element.33), calls=%async_computation | async-start | bytes 3145728 | tf_op jit(solution)/shard_map/all_to_all | solution.py:676
  15.1 4.1 %collective-permute-start.2 = (f32[2,2,3,2,2,16,128]{6,5,4,3,2,1,0:T(8,128)S(1)}, f32[2,2,3,2,2,16,128]{6,5,4,3,2,1,0:T(8,128)S(1)}, u32[]{:S(2)}, u32[]{:S(2)}) collective-permute-start(f32[2,2,3,2,2,16,128]{6,5,4,3,2,1,0:T(8,128)S(1)} %get-tuple-element.44), channel_id=1, source_target_pairs={{0,7},{1,0},{2,1},{3,2},{4,3},{5,4},{6,5},{7,6},{8,15},{9,8},{10,9... | collective-permute-start | bytes 1179656 | tf_op jit(solution)/shard_map/ppermute | solution.py:14
  19.2 5.2 %shard_map.51 = (f32[2,4,16,128]{3,2,1,0:T(8,128)S(1)}, f32[8,128]{1,0:T(8,128)S(1)}, f32[3,18,2,4,16,128]{5,4,3,2,1,0:T(8,128)S(1)}, f32[2,18,8,128]{3,2,1,0:T(8,128)S(1)}, f32[2,18,8,128]{3,2,1,0:T(8,128)S(1)}) custom-call(f32[4,3,3,2,2,4,16,128]{7,6,5,4,3,2,1,0:T(8,128)} %links_ref.4, f32[3,8,128]{2,1,0:T(8,128)S(1)} %collective-permute-done.x_ref, ...), custom_call_target="tpu_custom_call" | custom-call | tf_op jit(solution)/shard_map/pallas_call | solution.py:437
  24.4 0.0 copy-start
  24.4 0.1 collective-permute-done.2.z_ref
  24.5 1.8 %shard_map.52 = (f32[2,4,16,128]{3,2,1,0:T(8,128)}, f32[8,128]{1,0:T(8,128)S(1)}) custom-call(f32[2,4,16,128]{3,2,1,0:T(8,128)S(1)} %get-tuple-element.39.inner_ref, f32[8,128]{1,0:T(8,128)S(1)} %get-tuple-element.40.part_ref, f32[3,18,2,4,16,128]{5,4,3,2,1,0:T(8,128)S(1)} %get-tuple-element.41.unit, f32[2,18,8,128]{3,2,1,0:T(8,128)S(1)} %get-tuple-element.42.x_edge, ...), custom_call_target="tpu_custom_call" | custom-call | tf_op jit(solution)/shard_map/pallas_call | solution.py:479
  26.2 0.0 collective-permute-start.3
  26.3 1.2 %collective-permute-done.3 = f32[8,128]{1,0:T(8,128)S(1)} collective-permute-done((f32[8,128]{1,0:T(8,128)S(1)}, f32[8,128]{1,0:T(8,128)S(1)}, u32[]{:S(2)}, u32[]{:S(2)}) %collective-permute-start.3) | collective-permute-done | bytes 4128 | tf_op jit(solution)/shard_map/ppermute | solution.py:669
  27.4 3.5 %collective-permute-start.4 = (f32[8,128]{1,0:T(8,128)S(1)}, f32[8,128]{1,0:T(8,128)S(1)}, u32[]{:S(2)}, u32[]{:S(2)}) collective-permute-start(f32[8,128]{1,0:T(8,128)S(1)} %add.9), channel_id=1, source_target_pairs={{0,6},{1,7},{2,4},{3,5},{4,2},{5,3},{6,0},{7,1},{8,14},{9,15},{10,... | collective-permute-start | bytes 12296 | tf_op jit(solution)/shard_map/ppermute | solution.py:669
  30.9 1.6 %collective-permute-done.4 = f32[8,128]{1,0:T(8,128)S(1)} collective-permute-done((f32[8,128]{1,0:T(8,128)S(1)}, f32[8,128]{1,0:T(8,128)S(1)}, u32[]{:S(2)}, u32[]{:S(2)}) %collective-permute-start.4) | collective-permute-done | bytes 4128 | tf_op jit(solution)/shard_map/ppermute | solution.py:669
  32.5 0.0 collective-permute-start.5
  32.5 3.6 %collective-permute-done.5 = f32[8,128]{1,0:T(8,128)S(1)} collective-permute-done((f32[8,128]{1,0:T(8,128)S(1)}, f32[8,128]{1,0:T(8,128)S(1)}, u32[]{:S(2)}, u32[]{:S(2)}) %collective-permute-start.5) | collective-permute-done | bytes 4128 | tf_op jit(solution)/shard_map/ppermute | solution.py:669
  36.1 1.3 %shard_map.53 = f32[16,72,128]{2,1,0:T(8,128)} custom-call(f32[3,2,3,2,2,16,128]{6,5,4,3,2,1,0:T(8,128)S(1)} %get-tuple-element.34.rest, f32[1,2,3,2,2,16,128]{6,5,4,3,2,1,0:T(8,128)S(1)} %get-tuple-element.35.rest_3, f32[8,128]{1,0:T(8,128)S(1)} %add.11.total_ref), custom_call_target="tpu_custom_call" | custom-call | tf_op jit(solution)/shard_map/pallas_call | solution.py:248
  37.4 0.1 all-to-all-done.own_ref
  37.5 5.0 %all-to-all-start.1 = ((f32[16,72,128]{2,1,0:T(8,128)}), f32[16,72,128]{2,1,0:T(8,128)S(1)}, u32[]{:S(2)}, u32[]{:S(2)}) async-start(f32[16,72,128]{2,1,0:T(8,128)} %shard_map.53), calls=%async_computation.1 | async-start | bytes 1179648 | tf_op jit(solution)/shard_map/all_to_all | solution.py:676
  42.4 0.0 copy-done
  42.5 0.6 %shard_map.54 = (f32[16,4,8,128]{3,2,1,0:T(8,128)S(1)}, f32[16,4,8,128]{3,2,1,0:T(8,128)S(1)}) custom-call(s32[2,9]{1,0:T(2,128)S(1)} %copy-done, f32[16,4,48,128]{3,2,1,0:T(8,128)S(1)} %all-to-all-done.own_ref), custom_call_target="tpu_custom_call" | custom-call | tf_op jit(solution)/shard_map/pallas_call | solution.py:592
  43.1 0.6 %collective-permute-start.6 = (f32[16,4,8,128]{3,2,1,0:T(8,128)S(1)}, f32[16,4,8,128]{3,2,1,0:T(8,128)S(1)}, u32[]{:S(2)}, u32[]{:S(2)}) collective-permute-start(f32[16,4,8,128]{3,2,1,0:T(8,128)S(1)} %get-tuple-element.47), channel_id=1, source_target_pairs={{0,1},{1,0},{2,3},{3,2},{4,5},{5,4},{6,7},{7,6},{8,9},{9,8},{10,11... | collective-permute-start | bytes 786440 | tf_op jit(solution)/shard_map/ppermute | solution.py:697
  43.6 0.7 %collective-permute-start.7 = (f32[16,4,8,128]{3,2,1,0:T(8,128)S(1)}, f32[16,4,8,128]{3,2,1,0:T(8,128)S(1)}, u32[]{:S(2)}, u32[]{:S(2)}) collective-permute-start(f32[16,4,8,128]{3,2,1,0:T(8,128)S(1)} %get-tuple-element.48), channel_id=1, source_target_pairs={{0,0},{7,7},{1,2},{2,1},{3,4},{4,3},{5,6},{6,5},{8,8},{15,15},{9,1... | collective-permute-start | bytes 786440 | tf_op jit(solution)/shard_map/ppermute | solution.py:698
  44.3 3.0 %shard_map.55.refs_4_ = f32[72,2,6,16,128]{4,3,2,1,0:T(8,128)} custom-call(s32[2,9]{1,0:T(2,128)S(1)} %copy-done, f32[16,4,48,128]{3,2,1,0:T(8,128)S(1)} %all-to-all-done.own_ref), custom_call_target="tpu_custom_call" | custom-call | tf_op jit(solution)/shard_map/pallas_call | solution.py:564
  47.3 0.0 collective-permute-done.6.refs_1_
  47.3 0.0 collective-permute-done.7.refs_2_
  47.3 6.2 %all-to-all-done.1.refs_3_ = f32[16,72,128]{2,1,0:T(8,128)S(1)} async-done(((f32[16,72,128]{2,1,0:T(8,128)}), f32[16,72,128]{2,1,0:T(8,128)S(1)}, u32[]{:S(2)}, u32[]{:S(2)}) %all-to-all-start.1) | async-done | bytes 589856 | tf_op jit(solution)/shard_map/all_to_all | solution.py:676
  53.5 2.1 %shard_map.56 = (f32[72,2,6,16,128]{4,3,2,1,0:T(8,128)}, f32[1,1]{1,0:T(1,128)}) custom-call(s32[2,9]{1,0:T(2,128)S(1)} %copy-done, f32[16,4,8,128]{3,2,1,0:T(8,128)S(1)} %collective-permute-done.6.refs_1_, f32[16,4,8,128]{3,2,1,0:T(8,128)S(1)} %collective-permute-done.7.refs_2_, ...), custom_call_target="tpu_custom_call", output_to_operand_aliasing={{0}: (4, {})} | custom-call | tf_op jit(solution)/shard_map/pallas_call | solution.py:652
  (3 shorter events, 0.0 us)
Async XLA Ops:
  2.6 8.8 %collective-permute-start.1 = (f32[2,8,8,128]{3,2,1,0:T(8,128)S(1)}, f32[2,8,8,128]{3,2,1,0:T(8,128)S(1)}, u32[]{:S(2)}, u32[]{:S(2)}) collective-permute-start(f32[2,8,8,128]{3,2,1,0:T(8,128)S(1)} %get-tuple-element.31), channel_id=1, source_target_pairs={{0,24},{8,0},{16,8},{24,16},{1,25},{9,1},{17,9},{25,17},{2,26},{10... | collective-permute-start | bytes 196616 | tf_op jit(solution)/shard_map/ppermute | solution.py:14
  5.5 5.9 %collective-permute-start = (f32[3,8,128]{2,1,0:T(8,128)S(1)}, f32[3,8,128]{2,1,0:T(8,128)S(1)}, u32[]{:S(2)}, u32[]{:S(2)}) collective-permute-start(f32[3,8,128]{2,1,0:T(8,128)S(1)} %get-tuple-element.30), channel_id=1, source_target_pairs={{0,96},{32,0},{64,32},{96,64},{1,97},{33,1},{65,33},{97,65},{2,98}... | collective-permute-start | bytes 36872 | tf_op jit(solution)/shard_map/ppermute | solution.py:14
  11.4 26.1 %all-to-all-start = ((f32[16,4,48,128]{3,2,1,0:T(8,128)}), f32[16,4,48,128]{3,2,1,0:T(8,128)S(1)}, u32[]{:S(2)}, u32[]{:S(2)}) async-start(f32[16,4,48,128]{3,2,1,0:T(8,128)} %get-tuple-element.33), calls=%async_computation | async-start | bytes 3145728 | tf_op jit(solution)/shard_map/all_to_all | solution.py:676
  15.1 9.4 %collective-permute-start.2 = (f32[2,2,3,2,2,16,128]{6,5,4,3,2,1,0:T(8,128)S(1)}, f32[2,2,3,2,2,16,128]{6,5,4,3,2,1,0:T(8,128)S(1)}, u32[]{:S(2)}, u32[]{:S(2)}) collective-permute-start(f32[2,2,3,2,2,16,128]{6,5,4,3,2,1,0:T(8,128)S(1)} %get-tuple-element.44), channel_id=1, source_target_pairs={{0,7},{1,0},{2,1},{3,2},{4,3},{5,4},{6,5},{7,6},{8,15},{9,8},{10,9... | collective-permute-start | bytes 1179656 | tf_op jit(solution)/shard_map/ppermute | solution.py:14
  24.4 18.1 %copy-start = (s32[2,9]{1,0:T(2,128)S(1)}, s32[2,9]{1,0:T(2,128)}, u32[]{:S(2)}) copy-start(s32[2,9]{1,0:T(2,128)} %refs_0_.1) | copy-start | bytes 220
  26.2 1.2 %collective-permute-start.3 = (f32[8,128]{1,0:T(8,128)S(1)}, f32[8,128]{1,0:T(8,128)S(1)}, u32[]{:S(2)}, u32[]{:S(2)}) collective-permute-start(f32[8,128]{1,0:T(8,128)S(1)} %get-tuple-element.45), channel_id=1, source_target_pairs={{0,1},{1,0},{2,3},{3,2},{4,5},{5,4},{6,7},{7,6},{8,9},{9,8},{10,11... | collective-permute-start | bytes 12296 | tf_op jit(solution)/shard_map/ppermute | solution.py:669
  27.4 5.0 %collective-permute-start.4 = (f32[8,128]{1,0:T(8,128)S(1)}, f32[8,128]{1,0:T(8,128)S(1)}, u32[]{:S(2)}, u32[]{:S(2)}) collective-permute-start(f32[8,128]{1,0:T(8,128)S(1)} %add.9), channel_id=1, source_target_pairs={{0,6},{1,7},{2,4},{3,5},{4,2},{5,3},{6,0},{7,1},{8,14},{9,15},{10,... | collective-permute-start | bytes 12296 | tf_op jit(solution)/shard_map/ppermute | solution.py:669
  32.5 3.6 %collective-permute-start.5 = (f32[8,128]{1,0:T(8,128)S(1)}, f32[8,128]{1,0:T(8,128)S(1)}, u32[]{:S(2)}, u32[]{:S(2)}) collective-permute-start(f32[8,128]{1,0:T(8,128)S(1)} %add.10), channel_id=1, source_target_pairs={{0,2},{1,3},{2,0},{3,1},{4,6},{5,7},{6,4},{7,5},{8,10},{9,11},{10,... | collective-permute-start | bytes 12296 | tf_op jit(solution)/shard_map/ppermute | solution.py:669
  37.5 16.0 %all-to-all-start.1 = ((f32[16,72,128]{2,1,0:T(8,128)}), f32[16,72,128]{2,1,0:T(8,128)S(1)}, u32[]{:S(2)}, u32[]{:S(2)}) async-start(f32[16,72,128]{2,1,0:T(8,128)} %shard_map.53), calls=%async_computation.1 | async-start | bytes 1179648 | tf_op jit(solution)/shard_map/all_to_all | solution.py:676
  43.1 4.2 %collective-permute-start.6 = (f32[16,4,8,128]{3,2,1,0:T(8,128)S(1)}, f32[16,4,8,128]{3,2,1,0:T(8,128)S(1)}, u32[]{:S(2)}, u32[]{:S(2)}) collective-permute-start(f32[16,4,8,128]{3,2,1,0:T(8,128)S(1)} %get-tuple-element.47), channel_id=1, source_target_pairs={{0,1},{1,0},{2,3},{3,2},{4,5},{5,4},{6,7},{7,6},{8,9},{9,8},{10,11... | collective-permute-start | bytes 786440 | tf_op jit(solution)/shard_map/ppermute | solution.py:697
  43.6 3.6 %collective-permute-start.7 = (f32[16,4,8,128]{3,2,1,0:T(8,128)S(1)}, f32[16,4,8,128]{3,2,1,0:T(8,128)S(1)}, u32[]{:S(2)}, u32[]{:S(2)}) collective-permute-start(f32[16,4,8,128]{3,2,1,0:T(8,128)S(1)} %get-tuple-element.48), channel_id=1, source_target_pairs={{0,0},{7,7},{1,2},{2,1},{3,4},{4,3},{5,6},{6,5},{8,8},{15,15},{9,1... | collective-permute-start | bytes 786440 | tf_op jit(solution)/shard_map/ppermute | solution.py:698
